TPU v7x, 128 devices: a whole 4x4x4 slice. The times are simulated.
128 devices in a mesh: lat: 8 (over z, x_lo), lon: 16 (over x_hi, y, core).
Axes of the slice: x: 4 (x_hi: 2, x_lo: 2; x = x_hi * 2 + x_lo), y: 4, z: 4, core: 2. Of those that a mesh axis runs over, the one named last changes fastest.
Arguments:
- tokens: bfloat16 [96, 192, 2, 2048], P('lat', None, None, 'lon'), may hold values from -6 to 6
- upstream: bfloat16 [96, 192, 2, 2048], P('lat', 'lon'), may hold values from -6 to 6
- qkv_weight: bfloat16 [2048, 3072], P('lon'), may hold values from -1 to 1
- out_weight: bfloat16 [1024, 2048], P('lon'), may hold values from -0.1875 to 0.1875
Outputs:
- grad_tokens: bfloat16 [96, 192, 2, 2048], P('lat', None, None, 'lon')
- grad_qkv_w: float32 [8, 2048, 3072], P('lat', 'lon')
- grad_out_w: float32 [8, 1024, 2048], P('lat', 'lon')
All inputs are finite; a program needn't handle non-finite values.
Results may differ from a plain program's by a relative error of at most 0.017.
Values may be sent and summed in bfloat16 or wider, within the bound.
No kernel may reach another device: no remote copies, remote signals or barrier semaphores. Data moves between devices by JAX's collectives and lax.ppermute only.
A program may use at most 128 MiB of HBM per device.

v0:
```python
import functools

import jax
import jax.numpy as jnp
from jax import lax
from jax.experimental import pallas as pl
from jax.experimental.pallas import tpu as pltpu
from jax.sharding import PartitionSpec as P

HEAD_DIM = 64
WLAT = 12
WLON = 6
LEVELS = 2
WTOK = WLAT * WLON * LEVELS
PAIR = 2 * WTOK
HALF = WTOK // 2
D = 2048
NY = 4
MIB = 1024 * 1024

NEG_FILL = -1e30
EPSILON = 1e-05


def lon_of(xh, y, c):
    return (xh * NY + y) * 2 + c


COORDS = [(xh, y, c) for xh in range(2) for y in range(NY) for c in range(2)]


def swap_c(value):
    return lax.ppermute(value, "lon", [(lon_of(x, y, c), lon_of(x, y, 1 - c)) for x, y, c in COORDS])


def swap_x(value):
    return lax.ppermute(value, "lon", [(lon_of(x, y, c), lon_of(1 - x, y, c)) for x, y, c in COORDS])


def shift_y(value, by):
    return lax.ppermute(value, "lon", [(lon_of(x, y, c), lon_of(x, (y + by) % NY, c)) for x, y, c in COORDS])


def hop_z(value, by):
    rows, lons = lax.axis_size("lat"), lax.axis_size("lon")
    pairs = [
        (r * lons + i, (r + (2 * by if r % 2 == 0 else 0)) % rows * lons + i) for r in range(rows) for i in range(lons)
    ]
    return lax.ppermute(value, ("lat", "lon"), pairs)


def across(value, other):
    rows, lons = lax.axis_size("lat"), lax.axis_size("lon")
    pairs = [
        (r * lons + i, (r ^ 1) * lons + (lon_of(1 - i // 8, i // 2 % NY, i % 2) if other else i))
        for r in range(rows) for i in range(lons)
    ]
    return lax.ppermute(value, ("lat", "lon"), pairs)


def next_lon(value):
    return lax.ppermute(value, "lon", [(i, (i - 1) % 16) for i in range(16)])


def mm(a, b, dims):
    return lax.dot_general(a, b, (dims, ((), ())), preferred_element_type=jnp.float32)


def shape(dims, dtype=jnp.bfloat16):
    return jax.ShapeDtypeStruct(dims, dtype)


def whole(*dims):
    return pl.BlockSpec(dims, lambda *_: (0,) * len(dims))


def weight_split_kernel(s_ref, q_ref, o_ref, w_ref, out_ref):
    group = s_ref[0] * 2 + s_ref[1]
    for xh in range(2):
        for c in range(2):
            slot = group ^ (xh * 2 + c)
            for part in range(3):
                for pair in range(2):
                    lo = (part * 8 + xh * 4 + pair * 2) * 128 + c * 64
                    w_ref[slot, part * 2 + pair] = jnp.concatenate(
                        [q_ref[:, lo:lo + 64], q_ref[:, lo + 128:lo + 192]], axis=1)
    for i in range(8):
        out_ref[i] = jnp.concatenate(
            [o_ref[:, i * 256:i * 256 + 128], o_ref[:, i * 256 + 128:i * 256 + 256]], axis=0)


def weight_split(scalars, qkv_weight, out_weight):
    return pl.pallas_call(
        weight_split_kernel,
        grid_spec=pltpu.PrefetchScalarGridSpec(
            num_scalar_prefetch=1,
            grid=(1,),
            in_specs=[whole(128, 3072), whole(64, D)],
            out_specs=[whole(4, 6, 128, 128), whole(8, 128, 128)],
        ),
        out_shape=[shape((4, 6, 128, 128)), shape((8, 128, 128))],
        cost_estimate=pl.CostEstimate(flops=0, bytes_accessed=2 * 10**6, transcendentals=0),
        name="weight_split",
    )(scalars, qkv_weight, out_weight)


def weight_join_kernel(s_ref, a_ref, b_ref, c_ref, out_ref):
    group = s_ref[0] * 2 + s_ref[1]

    def block(slot, index):
        return jnp.where(slot == 0, a_ref[index], jnp.where(
            slot == 1, b_ref[0, index].astype(jnp.float32), jnp.where(
                slot == 3, b_ref[1, index], c_ref[0, index]).astype(jnp.float32)))

    for xh in range(2):
        slots = [group ^ (xh * 2), group ^ (xh * 2 + 1)]
        for part in range(3):
            for pair in range(2):
                left, right = (block(slot, part * 2 + pair) for slot in slots)
                lo = (part * 8 + xh * 4 + pair * 2) * 128
                out_ref[:, lo:lo + 128] = jnp.concatenate([left[:, :64], right[:, :64]], axis=1)
                out_ref[:, lo + 128:lo + 256] = jnp.concatenate([left[:, 64:], right[:, 64:]], axis=1)


def weight_join(scalars, own, by_c, by_x):
    return pl.pallas_call(
        weight_join_kernel,
        grid_spec=pltpu.PrefetchScalarGridSpec(
            num_scalar_prefetch=1,
            grid=(1,),
            in_specs=[whole(6, 128, 128), whole(2, 6, 128, 128), whole(2, 6, 128, 128)],
            out_specs=whole(128, 3072),
        ),
        out_shape=shape((128, 3072), jnp.float32),
        compiler_params=pltpu.CompilerParams(vmem_limit_bytes=60 * MIB),
        cost_estimate=pl.CostEstimate(flops=0, bytes_accessed=3 * 10**6, transcendentals=0),
        name="weight_join",
    )(scalars, own, by_c, by_x)


def spans(y):
    for s in range(4):
        for w in range(2):
            for t in range(4):
                xh, c = t // 2, t % 2
                start = 12 * lon_of(xh, lax.rem(y + s, 4), c) + 3 + 6 * w
                if xh == 1 and c == 1 and w == 1:
                    yield s, w, t, start, 0, 3
                    yield s, w, t, lax.rem(start + 3, 192), 3, 3
                else:
                    yield s, w, t, start, 0, 6


def token_split_kernel(s_ref, high_ref, low_ref, *outs):
    for s, w, t, start, offset, columns in spans(s_ref[2]):
        for half, ref in enumerate((high_ref, low_ref)):
            outs[s][half, w, t, :, offset:offset + columns] = ref[:, pl.ds(start, columns)]


def token_split(scalars, tokens, low):
    dims = (2, 2, 4, 6, WLON, LEVELS, 128)
    return pl.pallas_call(
        token_split_kernel,
        grid_spec=pltpu.PrefetchScalarGridSpec(
            num_scalar_prefetch=1,
            grid=(1,),
            in_specs=[
                pl.BlockSpec((6, 192, LEVELS, 128), lambda i, r: (1, 0, 0, 0)), whole(6, 192, LEVELS, 128),
            ],
            out_specs=[whole(*dims)] * 4,
        ),
        out_shape=[shape(dims)] * 4,
        compiler_params=pltpu.CompilerParams(vmem_limit_bytes=40 * MIB),
        cost_estimate=pl.CostEstimate(flops=0, bytes_accessed=3 * 10**6, transcendentals=0),
        name="token_split",
    )(scalars, tokens, low)


def token_join_kernel(s_ref, *refs):
    parts, out_ref = refs[:4], refs[4]
    for s, w, t, start, offset, columns in spans(s_ref[2]):
        out_ref[6:12, pl.ds(start, columns)] = parts[s][w, t, 0:6, offset:offset + columns]
        out_ref[0:6, pl.ds(start, columns)] = parts[s][w, t, 6:12, offset:offset + columns]


def token_join(scalars, parts):
    return pl.pallas_call(
        token_join_kernel,
        grid_spec=pltpu.PrefetchScalarGridSpec(
            num_scalar_prefetch=1,
            grid=(1,),
            in_specs=[whole(2, 4, WLAT, WLON, LEVELS, 128)] * 4,
            out_specs=whole(WLAT, 192, LEVELS, 128),
        ),
        out_shape=shape((WLAT, 192, LEVELS, 128)),
        compiler_params=pltpu.CompilerParams(vmem_limit_bytes=40 * MIB),
        cost_estimate=pl.CostEstimate(flops=0, bytes_accessed=3 * 10**6, transcendentals=0),
        name="token_join",
    )(scalars, *parts)


def attend(qkv, grad_att, split):
    scale = HEAD_DIM ** -0.5
    lane = lax.broadcasted_iota(jnp.int32, (1, 128), 1)
    row_group = lax.broadcasted_iota(jnp.int32, (WTOK, WTOK), 0) >= HALF
    col_group = lax.broadcasted_iota(jnp.int32, (WTOK, WTOK), 1) >= HALF
    keep = (row_group == col_group) | (split == 0)
    units = []
    for w in range(2):
        rows = slice(w * WTOK, (w + 1) * WTOK)
        for pair in range(2):
            cols = slice(pair * 128, (pair + 1) * 128)
            q = qkv[rows, 0:256][:, cols] * scale
            k = qkv[rows, 256:512][:, cols]
            v = qkv[rows, 512:768][:, cols]
            g = grad_att[rows, cols]
            heads = []
            for h in range(2):
                mine = (lane < 64) == (h == 0)
                heads.append((
                    jnp.where(mine, q, 0.0).astype(jnp.bfloat16),
                    jnp.where(mine, g, 0.0).astype(jnp.bfloat16),
                ))
            kb, vb = k.astype(jnp.bfloat16), v.astype(jnp.bfloat16)
            units.append((heads, kb, vb, k.T.astype(jnp.bfloat16), v.T.astype(jnp.bfloat16)))
    work = [(u, h) for u in range(4) for h in range(2)]
    scores = {
        (u, h): mm(units[u][1], units[u][0][h][0], ((1,), (1,))) for u, h in work
    }
    probs, probs_b = {}, {}
    for key in work:
        kept = jnp.where(keep, scores[key], NEG_FILL)
        expons = jnp.exp(kept - jnp.max(kept, axis=0, keepdims=True))
        probs[key] = expons * (1.0 / jnp.sum(expons, axis=0, keepdims=True))
        probs_b[key] = probs[key].astype(jnp.bfloat16)
    grads = {}
    for u, h in work:
        weighted = probs[u, h] * mm(units[u][2], units[u][0][h][1], ((1,), (1,)))
        inner = jnp.sum(weighted, axis=0, keepdims=True)
        grads[u, h] = (weighted - probs[u, h] * inner).astype(jnp.bfloat16)
    att, dq, dk, dv = [], [], [], []
    for u in range(4):
        heads, _, _, kt, vt = units[u]
        att.append(jnp.concatenate(
            [mm(vt[h * 64:(h + 1) * 64], probs_b[u, h], ((1,), (0,))) for h in range(2)], axis=0).T)
        dq.append(jnp.concatenate(
            [mm(kt[h * 64:(h + 1) * 64], grads[u, h], ((1,), (0,))) for h in range(2)], axis=0).T * scale)
        dk.append(sum(mm(grads[u, h], heads[h][0], ((1,), (0,))) for h in range(2)))
        dv.append(sum(mm(probs_b[u, h], heads[h][1], ((1,), (0,))) for h in range(2)))
    attended = jnp.concatenate([jnp.concatenate(att[2 * w:2 * w + 2], axis=1) for w in range(2)], axis=0)
    dqkv = jnp.concatenate([
        jnp.concatenate(dq[2 * w:2 * w + 2] + dk[2 * w:2 * w + 2] + dv[2 * w:2 * w + 2], axis=1)
        for w in range(2)], axis=0)
    return attended.astype(jnp.bfloat16), dqkv.astype(jnp.bfloat16)


ORDER = (2, 1, 3, 0)


def window_kernel(s_ref, *refs):
    highs, lows, us, ws = refs[:4], refs[4:8], refs[8:12], refs[12:17]
    pc_ref, px_ref, po_ref = refs[17:20]
    terms = refs[20:25]
    wfull, wout, ub, gacc, nb_all, dq_all, wsum, att_all = refs[25:]
    i = pl.program_id(0)
    c, y = s_ref[1], s_ref[2]

    @pl.when(i == 0)
    def _():
        for s in range(4):
            def block(index):
                if s == 2:
                    return ws[2][index] if index < 16 else ws[4][index - 16]
                return ws[s][index]
            for k in range(4):
                row = (s * 4 + k) * 128
                for part in range(6):
                    wfull[row:row + 128, part * 128:(part + 1) * 128] = block((0, 2, 1, 3)[k] * 6 + part)
            head = lax.rem(y + 4 - s, 4)
            rows = pl.ds(pl.multiple_of(head * 64, 64), 64)
            for j in range(8):
                wout[rows, j * 256:j * 256 + 128] = block(24 + j)[0:64]
                wout[rows, j * 256 + 128:j * 256 + 256] = block(24 + j)[64:128]
        wsum[...] = jnp.sum(wfull[...].astype(jnp.float32), axis=0, keepdims=True)

    rows = pl.ds(pl.multiple_of(i * PAIR, PAIR), PAIR)
    for step in range(4):
        @pl.when(i == step)
        def _():
            for dc in range(2):
                ub[pl.ds(pl.multiple_of(step * PAIR + (dc ^ c) * WTOK, WTOK), WTOK), :] = us[2 * (step % 2) + dc][0]

    x = jnp.concatenate([
        jnp.concatenate(
            [half[k][s, 0].astype(jnp.float32) for half in (highs, lows)], axis=1).reshape(PAIR, 128)
        for s in range(4) for k in range(4)
    ], axis=1)
    centred = x - jnp.mean(x, axis=-1, keepdims=True)
    inverse = lax.rsqrt(jnp.mean(centred * centred, axis=-1, keepdims=True) + EPSILON)
    nb = (centred * inverse).astype(jnp.bfloat16)
    nb_all[rows, :] = nb
    qkv = mm(nb, wfull[...], ((1,), (0,)))
    grad_att = mm(ub[rows, :], wout[...], ((1,), (1,)))
    attended, dqkv = attend(qkv, grad_att, s_ref[3])
    att_all[rows, :] = attended
    dq_all[rows, :] = dqkv
    dqkv_f = dqkv.astype(jnp.float32)
    mean_one = jnp.sum(dqkv_f * wsum[...], axis=-1, keepdims=True) * (inverse / D)
    mean_two = jnp.sum(dqkv_f * qkv, axis=-1, keepdims=True) * (inverse / D)
    grad_normal = mm(dqkv, wfull[...], ((1,), (1,)))
    normal = nb_all[rows, :].astype(jnp.float32)
    grad_rolled = inverse * grad_normal - mean_one - normal * mean_two

    for s in range(4):
        part = [grad_rolled[:, (s * 4 + k) * 128:(s * 4 + k + 1) * 128].reshape(2, WTOK, 128) for k in range(4)]
        pc_ref[0, s, 0] = part[1].astype(jnp.bfloat16)
        pc_ref[1, s, 0] = part[3].astype(jnp.bfloat16)
        px_ref[s, 0] = part[2].astype(jnp.bfloat16)
        block = lon_of(s_ref[0], lax.rem(y + 4 - s, 4), c)
        own = ub[rows, pl.ds(pl.multiple_of(block * 128, 128), 128)].astype(jnp.float32)
        po_ref[s, 0] = (part[0] + own.reshape(2, WTOK, 128)).astype(jnp.bfloat16)

    @pl.when(i == 3)
    def _():
        gacc[...] = mm(att_all[...], ub[...], ((0,), (0,)))
        for step, s in enumerate(ORDER):
            places = {2: ((0, 0), (1, 16)), 1: ((2, 0), (0, 16)), 3: ((1, 0), (3, 0)), 0: ((4, 0), (4, 16))}[s]

            def put(index, value):
                at, offset = places[index // 16]
                terms[at][offset + index % 16] = value.astype(jnp.bfloat16)

            term = mm(nb_all[:, s * 512:(s + 1) * 512], dq_all[...], ((0,), (0,)))
            for k in range(4):
                for part in range(6):
                    put(k * 6 + part, term[k * 128:(k + 1) * 128, part * 128:(part + 1) * 128])
            head = lax.rem(y + 4 - s, 4)
            gw = gacc[pl.ds(pl.multiple_of(head * 64, 64), 64), :]
            for j in range(8):
                put(24 + j, jnp.concatenate(
                    [gw[:, j * 256:j * 256 + 128], gw[:, j * 256 + 128:j * 256 + 256]], axis=0))


def once(*dims):
    return pl.BlockSpec(dims, lambda *_: (0,) * len(dims), pipeline_mode=pl.Buffered(1))


def window_pass(scalars, xs, us, ws):
    sizes = [32, 32, 16, 16, 32]
    dtypes = [jnp.bfloat16] * 5
    tile = pl.BlockSpec((4, 1, 2, WTOK, 128), lambda i, s: (0, i // 2, (i % 2) ^ s[0], 0, 0))
    part_specs = [
        pl.BlockSpec((2, 4, 1, 2, WTOK, 128), lambda i, s: (0, 0, i // 2, (i % 2) ^ s[0], 0, 0)), tile, tile,
    ]
    part_shapes = [
        shape((2, 4, 2, 4, WTOK, 128)), shape((4, 2, 4, WTOK, 128)), shape((4, 2, 4, WTOK, 128)),
    ]
    return pl.pallas_call(
        window_kernel,
        grid_spec=pltpu.PrefetchScalarGridSpec(
            num_scalar_prefetch=1,
            grid=(4,),
            in_specs=[
                pl.BlockSpec((4, 1, 2, HALF, 128), lambda i, s: (0, i // 2, (i % 2) ^ s[0], 0, 0))
            ] * 8 + [pl.BlockSpec((1, WTOK, D), lambda i, s: (i // 2, 0, 0))] * 4
            + [once(n, 128, 128) for n in (32, 32, 16, 32, 16)],
            out_specs=part_specs + [once(n, 128, 128) for n in sizes],
            scratch_shapes=[
                pltpu.VMEM((D, 768), jnp.bfloat16),
                pltpu.VMEM((256, D), jnp.bfloat16),
                pltpu.VMEM((4 * PAIR, D), jnp.bfloat16),
                pltpu.VMEM((256, D), jnp.float32),
                pltpu.VMEM((4 * PAIR, D), jnp.bfloat16),
                pltpu.VMEM((4 * PAIR, 768), jnp.bfloat16),
                pltpu.VMEM((1, 768), jnp.float32),
                pltpu.VMEM((4 * PAIR, 256), jnp.bfloat16),
            ],
        ),
        out_shape=part_shapes + [shape((n, 128, 128), t) for n, t in zip(sizes, dtypes)],
        compiler_params=pltpu.CompilerParams(vmem_limit_bytes=40 * MIB),
        cost_estimate=pl.CostEstimate(flops=32 * 10**9, bytes_accessed=30 * 10**6, transcendentals=10**6),
        name="window_pass",
    )(scalars, *xs, *us, *ws)


def after(values, *earlier):
    return lax.optimization_barrier(tuple(values) + earlier)[:len(values)]


def local(tokens, upstream, qkv_weight, out_weight):
    lon = lax.axis_index("lon")
    lat = lax.axis_index("lat")
    xh, y, c = lon // 8, (lon // 2) % 4, lon % 2
    last = (lat == lax.axis_size("lat") - 1).astype(jnp.int32)
    scalars = jnp.stack([jnp.int32(v) for v in (xh, c, y, last)])

    split, out_blocks = weight_split(scalars, qkv_weight, out_weight)
    token_low = hop_z(tokens[:6], -1)
    (upstream,) = after((upstream,), out_blocks)
    from_x = swap_x(jnp.stack([split[2], split[3]]))
    next_cols = next_lon(upstream[:, :3])

    cols = jnp.concatenate([upstream[:, 3:], next_cols], axis=1)
    cols = cols.reshape(2, 6, 2, WLON, LEVELS, D).transpose(0, 2, 1, 3, 4, 5).reshape(2, 2, HALF, D)
    pieces = token_split(scalars, tokens, token_low)
    u_low, u_high, *pieces = after((cols[0], cols[1], *pieces))
    from_c = swap_c(jnp.stack([split[1], from_x[1]]))
    u_x = [swap_x(u_high)]
    u_low = hop_z(u_low, -1)
    pieces = [pieces[0]] + [shift_y(pieces[s], s) for s in (1, 2, 3)]
    x_high = jnp.stack([piece[0] for piece in pieces]).reshape(4, 2, 4, HALF, 128)
    x_low = jnp.stack([piece[1] for piece in pieces]).reshape(4, 2, 4, HALF, 128)

    shard = jnp.concatenate([split[0], from_x[0], from_c.reshape(12, 128, 128), out_blocks])
    shard, u_low, x_high, x_low = after((shard, u_low, x_high, x_low), from_c, u_low, u_x[0], *pieces[1:])
    w_up, w_down = shift_y(shard, 1), shift_y(shard, -1)
    u_x.append(across(u_low, True))
    u_own = [u_high, across(u_low, False)]
    highs = [x_high, swap_c(x_high), swap_x(x_high)]

    up_half, down_half, x_low = after(
        (w_up[:16], w_down[16:], x_low), w_up, w_down, u_x[1], u_own[1], highs[2])
    ws = [shard, w_up, shift_y(up_half, 1), w_down, shift_y(down_half, -1)]
    lows = [across(x_low, False), across(x_low, True)]
    u_own, u_x = (jnp.concatenate(u, axis=1) for u in (u_own, u_x))
    us = [u_own, swap_c(u_own), u_x]

    lows[0], lows[1], to_c, u_x = after((*lows, highs[2], u_x), ws[2], ws[4], highs[1], us[1])
    us.append(swap_c(u_x))
    highs.append(swap_c(to_c))
    lows = [lows[0], swap_c(lows[0]), lows[1], swap_c(lows[1])]

    xs = highs + lows
    part_c, part_x, part_own, lower, upper, up, down, mine = window_pass(scalars, xs, us, ws)

    def plus(a, b):
        return (a.astype(jnp.float32) + b.astype(jnp.float32)).astype(jnp.bfloat16)

    got_c = swap_c(part_c)
    own = part_own.astype(jnp.float32) + got_c[0].astype(jnp.float32)
    other = plus(part_x, got_c[1])

    lower, upper = shift_y(lower, -1), shift_y(upper, 1)
    low = [across(own[..., HALF:, :].astype(jnp.bfloat16), False), across(other[..., HALF:, :], True)]

    high, low = after((other[..., :HALF, :], plus(*low)), *low)
    up, down = after((plus(up, lower[:16]), plus(down, upper[16:])), lower, upper, high, low)
    high = (own[..., :HALF, :] + swap_x(high).astype(jnp.float32)).astype(jnp.bfloat16)
    low = hop_z(low, 1)
    up, down = shift_y(up, -1), shift_y(down, 1)

    total = mine.astype(jnp.float32) + jnp.concatenate([up, lower[16:]]).astype(jnp.float32) + jnp.concatenate(
        [upper[:16], down]).astype(jnp.float32)
    full = jnp.concatenate([high, low], axis=3)
    (total,) = after((total,), full)
    back = [full[0]] + [shift_y(full[s], -s) for s in (1, 2, 3)]
    blocks = total[:24].reshape(4, 6, 128, 128)
    sent = blocks.astype(jnp.bfloat16)
    by_x = swap_x(sent[2:])
    (near_x,) = after((by_x,), *back[1:])
    by_c = swap_c(jnp.stack([sent[1], near_x[1]]))
    grad_qkv_w = weight_join(scalars, total, by_c, by_x)
    grad_out_w = total[24:].reshape(8, 2, 64, 128).transpose(2, 0, 1, 3).reshape(64, D)

    result = token_join(scalars, [b.reshape(2, 4, WLAT, WLON, LEVELS, 128) for b in back])
    return (result, grad_qkv_w[None], grad_out_w[None])


def solution(mesh):
    return jax.shard_map(
        local,
        mesh=mesh,
        in_specs=(
            P("lat", None, None, "lon"),
            P("lat", "lon", None, None),
            P("lon", None),
            P("lon", None),
        ),
        out_specs=(P("lat", None, None, "lon"), P("lat", "lon", None), P("lat", "lon", None)),
        check_vma=False,
    )
```

profile of v0, /device:TPU:1, one launch (start us, length us, event | category | flops | bytes accessed | tf_op | source)
XLA Modules:
  0.0 207.6 jit_solution(11232417979571816268)
XLA Ops:
  0.7 0.6 pad_add_fusion.s_ref
  1.3 3.1 %weight_split.1 = (bf16[4,6,128,128]{3,2,1,0:T(8,128)(2,1)}, bf16[8,128,128]{2,1,0:T(8,128)(2,1)}) custom-call(s32[4]{0:T(128)} %pad_add_fusion.s_ref, bf16[128,3072]{1,0:T(8,128)(2,1)} %q_ref.1, bf16[64,2048]{1,0:T(8,128)(2,1)} %o_ref.1), custom_call_target="tpu_custom_call" | custom-call | bytes 2000000 | tf_op jit(solution)/shard_map/weight_split/pallas_call | solution.py:93
  4.4 1.2 slice.132
  5.6 1.5 collective-permute-start.2
  7.1 1.2 slice.135
  8.4 5.7 %collective-permute-start.3 = (bf16[6,192,2,128]{3,2,1,0:T(2,128)(2,1)}, bf16[6,192,2,128]{3,2,1,0:T(2,128)(2,1)S(1)}, u32[]{:S(2)}, u32[]{:S(2)}) collective-permute-start(bf16[6,192,2,128]{3,2,1,0:T(2,128)(2,1)} %slice.135), channel_id=1, source_target_pairs={{0,96},{1,97},{2,98},{3,99},{4,100},{5,101},{6,102},{7,103},{8,104... | collective-permute-start | bytes 1769480 | tf_op jit(solution)/shard_map/ppermute | solution.py:49
  14.2 2.8 %collective-permute-start = (bf16[2,6,128,128]{3,2,1,0:T(8,128)(2,1)S(1)}, bf16[2,6,128,128]{3,2,1,0:T(8,128)(2,1)S(1)}, u32[]{:S(2)}, u32[]{:S(2)}) collective-permute-start(bf16[2,6,128,128]{3,2,1,0:T(8,128)(2,1)S(1)} %stack.39), channel_id=1, source_target_pairs={{0,8},{1,9},{2,10},{3,11},{4,12},{5,13},{6,14},{7,15},{8,0},{9,1},... | collective-permute-start | bytes 1179656 | tf_op jit(solution)/shard_map/ppermute | solution.py:37
  17.0 0.7 slice_bitcast_fusion.4
  17.7 1.5 pad_maximum_fusion.1
  19.2 1.0 copy.10
  20.2 2.5 %collective-permute-done = bf16[2,6,128,128]{3,2,1,0:T(8,128)(2,1)S(1)} collective-permute-done((bf16[2,6,128,128]{3,2,1,0:T(8,128)(2,1)S(1)}, bf16[2,6,128,128]{3,2,1,0:T(8,128)(2,1)S(1)}, u32[]{:S(2)}, u32[]{:S(2)}) %collective-permute-start) | collective-permute-done | bytes 393248 | tf_op jit(solution)/shard_map/ppermute | solution.py:37
  22.7 0.7 slice_bitcast_fusion.3
  23.4 0.8 pad_maximum_fusion.5
  24.2 6.0 %collective-permute-start.1 = (bf16[2,6,128,128]{3,2,1,0:T(8,128)(2,1)}, bf16[2,6,128,128]{3,2,1,0:T(8,128)(2,1)}, u32[]{:S(2)}, u32[]{:S(2)}) collective-permute-start(bf16[2,6,128,128]{3,2,1,0:T(8,128)(2,1)} %pad_maximum_fusion.5), channel_id=1, source_target_pairs={{0,1},{1,0},{2,3},{3,2},{4,5},{5,4},{6,7},{7,6},{8,9},{9,8},{10,11... | collective-permute-start | bytes 1179656 | tf_op jit(solution)/shard_map/ppermute | solution.py:33
  30.2 1.0 fusion.10
  31.9 0.9 token_split.1
  32.8 2.5 %collective-permute-start.6 = (bf16[2,2,4,6,6,2,128]{6,5,4,3,2,1,0:T(2,128)(2,1)S(1)}, bf16[2,2,4,6,6,2,128]{6,5,4,3,2,1,0:T(2,128)(2,1)S(1)}, u32[]{:S(2)}, u32[]{:S(2)}) collective-permute-start(bf16[2,2,4,6,6,2,128]{6,5,4,3,2,1,0:T(2,128)(2,1)S(1)} %get-tuple-element.51), channel_id=1, source_target_pairs={{0,4},{1,5},{2,6},{3,7},{4,0},{5,1},{6,2},{7,3},{8,12},{9,13},{10,... | collective-permute-start | bytes 884744 | tf_op jit(solution)/shard_map/ppermute | solution.py:41
  35.3 1.1 collective-permute-start.7
  36.4 2.0 collective-permute-start.4
  38.6 2.8 %collective-permute-start.8 = (bf16[2,72,2048]{2,1,0:T(8,128)(2,1)S(1)}, bf16[2,72,2048]{2,1,0:T(8,128)(2,1)S(1)}, u32[]{:S(2)}, u32[]{:S(2)}) collective-permute-start(bf16[2,72,2048]{2,1,0:T(8,128)(2,1)S(1)} %squeeze.26), channel_id=1, source_target_pairs={{0,8},{1,9},{2,10},{3,11},{4,12},{5,13},{6,14},{7,15},{8,0},{9,1},... | collective-permute-start | bytes 1769480 | tf_op jit(solution)/shard_map/ppermute | solution.py:37
  41.5 1.1 pad_maximum_fusion.2.refs_12_
  43.1 5.8 %collective-permute-done.6 = bf16[2,2,4,6,6,2,128]{6,5,4,3,2,1,0:T(2,128)(2,1)S(1)} collective-permute-done((bf16[2,2,4,6,6,2,128]{6,5,4,3,2,1,0:T(2,128)(2,1)S(1)}, bf16[2,2,4,6,6,2,128]{6,5,4,3,2,1,0:T(2,128)(2,1)S(1)}, u32[]{:S(2)}, u32[]{:S(2)}) %collective-permute-start.6) | collective-permute-done | bytes 294944 | tf_op jit(solution)/shard_map/ppermute | solution.py:41
  49.5 2.2 %pad_maximum_fusion.3 = (bf16[4,2,4,6,6,2,128]{6,5,4,3,2,1,0:T(2,128)(2,1)S(1)}, bf16[4,2,4,6,6,2,128]{6,5,4,3,2,1,0:T(2,128)(2,1)S(1)}) fusion(bf16[1,2,4,6,6,2,128]{6,5,4,3,2,1,0:T(2,128)(2,1)S(1)} %get-tuple-element.100, bf16[1,2,4,6,6,2,128]{6,5,4,3,2,1,0:T(2,128)(2,1)S(1)} %get-tuple-element.98, ...), kind=kLoop, calls=%fused_computation.24 | loop fusion | flops 1769472 | bytes 2359296 | tf_op jit(solution)/shard_map/stack | solution.py:411
  51.7 0.6 collective-permute-done.4
  52.3 1.0 collective-permute-done.8
  53.2 1.5 collective-permute-start.12
  54.8 3.0 %collective-permute-start.13 = (bf16[2,72,2048]{2,1,0:T(8,128)(2,1)S(1)}, bf16[2,72,2048]{2,1,0:T(8,128)(2,1)S(1)}, u32[]{:S(2)}, u32[]{:S(2)}) collective-permute-start(bf16[2,72,2048]{2,1,0:T(8,128)(2,1)S(1)} %collective-permute-done.4), channel_id=1, source_target_pairs={{0,24},{1,25},{2,26},{3,27},{4,28},{5,29},{6,30},{7,31},{8,16},{9,... | collective-permute-start | bytes 1769480 | tf_op jit(solution)/shard_map/ppermute | solution.py:58
  58.1 9.5 %collective-permute-done.14 = bf16[2,72,2048]{2,1,0:T(8,128)(2,1)S(1)} collective-permute-done((bf16[2,72,2048]{2,1,0:T(8,128)(2,1)S(1)}, bf16[2,72,2048]{2,1,0:T(8,128)(2,1)S(1)}, u32[]{:S(2)}, u32[]{:S(2)}) %collective-permute-start.14) | collective-permute-done | bytes 589856 | tf_op jit(solution)/shard_map/ppermute | solution.py:58
  67.7 5.6 %collective-permute-start.19 = (bf16[2,144,2048]{2,1,0:T(8,128)(2,1)S(1)}, bf16[2,144,2048]{2,1,0:T(8,128)(2,1)S(1)}, u32[]{:S(2)}, u32[]{:S(2)}) collective-permute-start(bf16[2,144,2048]{2,1,0:T(8,128)(2,1)S(1)} %constant_dynamic-update-slice_fusion.2.refs_8_), channel_id=1, source_target_pairs={{0,1},{1,0},{2,3},{3,2},{4,5},{5,4},{6,7},{7,6},{8,9},{9,8},{10,11... | collective-permute-start | bytes 3538952 | tf_op jit(solution)/shard_map/ppermute | solution.py:33
  73.3 2.2 %collective-permute-done.12.refs_15_ = bf16[32,128,128]{2,1,0:T(8,128)(2,1)S(1)} collective-permute-done((bf16[32,128,128]{2,1,0:T(8,128)(2,1)S(1)}, bf16[32,128,128]{2,1,0:T(8,128)(2,1)S(1)}, u32[]{:S(2)}, u32[]{:S(2)}) %collective-permute-start.12) | collective-permute-done | bytes 1048608 | tf_op jit(solution)/shard_map/ppermute | solution.py:41
  75.5 3.3 %collective-permute-start.9 = (bf16[4,2,4,72,128]{4,3,2,1,0:T(8,128)(2,1)S(1)}, bf16[4,2,4,72,128]{4,3,2,1,0:T(8,128)(2,1)S(1)}, u32[]{:S(2)}, u32[]{:S(2)}) collective-permute-start(bf16[4,2,4,72,128]{4,3,2,1,0:T(8,128)(2,1)S(1)} %bitcast.44), channel_id=1, source_target_pairs={{0,1},{1,0},{2,3},{3,2},{4,5},{5,4},{6,7},{7,6},{8,9},{9,8},{10,11... | collective-permute-start | bytes 1769480 | tf_op jit(solution)/shard_map/ppermute | solution.py:33
  78.9 2.4 %collective-permute-done.10.refs_2_ = bf16[4,2,4,72,128]{4,3,2,1,0:T(8,128)(2,1)S(1)} collective-permute-done((bf16[4,2,4,72,128]{4,3,2,1,0:T(8,128)(2,1)S(1)}, bf16[4,2,4,72,128]{4,3,2,1,0:T(8,128)(2,1)S(1)}, u32[]{:S(2)}, u32[]{:S(2)}) %collective-permute-start.10) | collective-permute-done | bytes 589856 | tf_op jit(solution)/shard_map/ppermute | solution.py:37
  81.3 1.4 collective-permute-start.16
  82.7 2.7 %collective-permute-start.18 = (bf16[16,128,128]{2,1,0:T(8,128)(2,1)S(1)}, bf16[16,128,128]{2,1,0:T(8,128)(2,1)S(1)}, u32[]{:S(2)}, u32[]{:S(2)}) collective-permute-start(bf16[16,128,128]{2,1,0:T(8,128)(2,1)S(1)} %slice.177), channel_id=1, source_target_pairs={{0,6},{1,7},{2,0},{3,1},{4,2},{5,3},{6,4},{7,5},{8,14},{9,15},{10,... | collective-permute-start | bytes 1572872 | tf_op jit(solution)/shard_map/ppermute | solution.py:41
  85.5 6.7 %collective-permute-done.17.refs_14_ = bf16[16,128,128]{2,1,0:T(8,128)(2,1)S(1)} collective-permute-done((bf16[16,128,128]{2,1,0:T(8,128)(2,1)S(1)}, bf16[16,128,128]{2,1,0:T(8,128)(2,1)S(1)}, u32[]{:S(2)}, u32[]{:S(2)}) %collective-permute-start.17) | collective-permute-done | bytes 524320 | tf_op jit(solution)/shard_map/ppermute | solution.py:41
  92.3 1.5 collective-permute-done.16.refs_6_
  93.8 7.1 %collective-permute-start.23 = (bf16[2,144,2048]{2,1,0:T(8,128)(2,1)S(1)}, bf16[2,144,2048]{2,1,0:T(8,128)(2,1)S(1)}, u32[]{:S(2)}, u32[]{:S(2)}) collective-permute-start(bf16[2,144,2048]{2,1,0:T(8,128)(2,1)S(1)} %constant_dynamic-update-slice_fusion.refs_10_), channel_id=1, source_target_pairs={{0,1},{1,0},{2,3},{3,2},{4,5},{5,4},{6,7},{7,6},{8,9},{9,8},{10,11... | collective-permute-start | bytes 3538952 | tf_op jit(solution)/shard_map/ppermute | solution.py:33
  101.5 2.7 %collective-permute-done.20.refs_3_ = bf16[4,2,4,72,128]{4,3,2,1,0:T(8,128)(2,1)S(1)} collective-permute-done((bf16[4,2,4,72,128]{4,3,2,1,0:T(8,128)(2,1)S(1)}, bf16[4,2,4,72,128]{4,3,2,1,0:T(8,128)(2,1)S(1)}, u32[]{:S(2)}, u32[]{:S(2)}) %collective-permute-start.20) | collective-permute-done | bytes 589856 | tf_op jit(solution)/shard_map/ppermute | solution.py:33
  104.2 0.8 collective-permute-done.21.refs_5_
  105.1 0.8 collective-permute-done.22.refs_7_
  105.9 1.1 copy-done.13
  107.0 28.9 %window_pass.1 = (bf16[2,4,2,4,144,128]{5,4,3,2,1,0:T(8,128)(2,1)}, bf16[4,2,4,144,128]{4,3,2,1,0:T(8,128)(2,1)S(1)}, bf16[4,2,4,144,128]{4,3,2,1,0:T(8,128)(2,1...) custom-call(s32[4]{0:T(128)S(1)} %copy-done.1, ...), custom_call_target="tpu_custom_call" | custom-call | flops 32000000000 | bytes 30000000 | tf_op jit(solution)/shard_map/window_pass/pallas_call | solution.py:358
  136.2 1.5 collective-permute-start.32
  137.7 3.0 %collective-permute-done.24 = bf16[2,4,2,4,144,128]{5,4,3,2,1,0:T(8,128)(2,1)S(1)} collective-permute-done((bf16[2,4,2,4,144,128]{5,4,3,2,1,0:T(8,128)(2,1)}, bf16[2,4,2,4,144,128]{5,4,3,2,1,0:T(8,128)(2,1)S(1)}, u32[]{:S(2)}, u32[]{:S(2)}) %collective-permute-start.24) | collective-permute-done | bytes 2359328 | tf_op jit(solution)/shard_map/ppermute | solution.py:33
  140.6 1.8 fusion
  142.6 1.8 collective-permute-start.25
  144.6 16.1 %collective-permute-done.32 = bf16[32,128,128]{2,1,0:T(8,128)(2,1)S(1)} collective-permute-done((bf16[32,128,128]{2,1,0:T(8,128)(2,1)S(1)}, bf16[32,128,128]{2,1,0:T(8,128)(2,1)S(1)}, u32[]{:S(2)}, u32[]{:S(2)}) %collective-permute-start.32) | collective-permute-done | bytes 1048608 | tf_op jit(solution)/shard_map/ppermute | solution.py:41
  160.8 2.3 %collective-permute-done.33 = bf16[32,128,128]{2,1,0:T(8,128)(2,1)S(1)} collective-permute-done((bf16[32,128,128]{2,1,0:T(8,128)(2,1)S(1)}, bf16[32,128,128]{2,1,0:T(8,128)(2,1)S(1)}, u32[]{:S(2)}, u32[]{:S(2)}) %collective-permute-start.33) | collective-permute-done | bytes 1048608 | tf_op jit(solution)/shard_map/ppermute | solution.py:41
  164.0 1.0 collective-permute-start.35
  165.0 1.2 collective-permute-start.27
  166.2 4.4 %collective-permute-start.28 = (bf16[4,2,4,72,128]{4,3,2,1,0:T(8,128)(2,1)S(1)}, bf16[4,2,4,72,128]{4,3,2,1,0:T(8,128)(2,1)S(1)}, u32[]{:S(2)}, u32[]{:S(2)}) collective-permute-start(bf16[4,2,4,72,128]{4,3,2,1,0:T(8,128)(2,1)S(1)} %add_convert_fusion), channel_id=1, source_target_pairs={{0,32},{1,33},{2,34},{3,35},{4,36},{5,37},{6,38},{7,39},{8,40},{9,... | collective-permute-start | bytes 1769480 | tf_op jit(solution)/shard_map/ppermute | solution.py:49
  170.7 4.9 %collective-permute-done.34 = bf16[16,128,128]{2,1,0:T(8,128)(2,1)S(1)} collective-permute-done((bf16[16,128,128]{2,1,0:T(8,128)(2,1)S(1)}, bf16[16,128,128]{2,1,0:T(8,128)(2,1)S(1)}, u32[]{:S(2)}, u32[]{:S(2)}) %collective-permute-start.34) | collective-permute-done | bytes 524320 | tf_op jit(solution)/shard_map/ppermute | solution.py:41
  175.6 1.7 collective-permute-done.35
  178.1 1.3 collective-permute-start.36
  179.6 2.4 %collective-permute-done.28 = bf16[4,2,4,72,128]{4,3,2,1,0:T(8,128)(2,1)S(1)} collective-permute-done((bf16[4,2,4,72,128]{4,3,2,1,0:T(8,128)(2,1)S(1)}, bf16[4,2,4,72,128]{4,3,2,1,0:T(8,128)(2,1)S(1)}, u32[]{:S(2)}, u32[]{:S(2)}) %collective-permute-start.28) | collective-permute-done | bytes 589856 | tf_op jit(solution)/shard_map/ppermute | solution.py:49
  182.4 2.4 %collective-permute-start.29 = (bf16[2,4,144,128]{3,2,1,0:T(8,128)(2,1)S(1)}, bf16[2,4,144,128]{3,2,1,0:T(8,128)(2,1)S(1)}, u32[]{:S(2)}, u32[]{:S(2)}) collective-permute-start(bf16[2,4,144,128]{3,2,1,0:T(8,128)(2,1)S(1)} %get-tuple-element.82), channel_id=1, source_target_pairs={{0,6},{1,7},{2,0},{3,1},{4,2},{5,3},{6,4},{7,5},{8,14},{9,15},{10,... | collective-permute-start | bytes 884744 | tf_op jit(solution)/shard_map/ppermute | solution.py:41
  185.3 3.9 %collective-permute-done.31 = bf16[2,4,144,128]{3,2,1,0:T(8,128)(2,1)S(1)} collective-permute-done((bf16[2,4,144,128]{3,2,1,0:T(8,128)(2,1)S(1)}, bf16[2,4,144,128]{3,2,1,0:T(8,128)(2,1)S(1)}, u32[]{:S(2)}, u32[]{:S(2)}) %collective-permute-start.31) | collective-permute-done | bytes 294944 | tf_op jit(solution)/shard_map/ppermute | solution.py:41
  189.2 1.3 collective-permute-done.29
  190.5 5.1 %collective-permute-done.30 = bf16[2,4,144,128]{3,2,1,0:T(8,128)(2,1)S(1)} collective-permute-done((bf16[2,4,144,128]{3,2,1,0:T(8,128)(2,1)S(1)}, bf16[2,4,144,128]{3,2,1,0:T(8,128)(2,1)S(1)}, u32[]{:S(2)}, u32[]{:S(2)}) %collective-permute-start.30) | collective-permute-done | bytes 294944 | tf_op jit(solution)/shard_map/ppermute | solution.py:41
  195.7 4.1 %collective-permute-start.37 = (bf16[2,6,128,128]{3,2,1,0:T(8,128)(2,1)S(1)}, bf16[2,6,128,128]{3,2,1,0:T(8,128)(2,1)S(1)}, u32[]{:S(2)}, u32[]{:S(2)}) collective-permute-start(bf16[2,6,128,128]{3,2,1,0:T(8,128)(2,1)S(1)} %pad_maximum_fusion.6), channel_id=1, source_target_pairs={{0,1},{1,0},{2,3},{3,2},{4,5},{5,4},{6,7},{7,6},{8,9},{9,8},{10,11... | collective-permute-start | bytes 1179656 | tf_op jit(solution)/shard_map/ppermute | solution.py:33
  200.2 1.2 broadcast_in_dim_reshape.3
  201.4 1.9 token_join.1
  203.3 0.7 copy-done.8
  204.1 3.5 %weight_join.1 = f32[128,3072]{1,0:T(8,128)} custom-call(s32[4]{0:T(128)} %pad_add_fusion.s_ref, f32[32,128,128]{2,1,0:T(8,128)} %copy-done.2, bf16[2,6,128,128]{3,2,1,0:T(8,128)(2,1)} %copy-done.8, bf16[2,6,128,128]{3,2,1,0:T(8,128)(2,1)} %copy-done.4), custom_call_target="tpu_custom_call" | custom-call | bytes 3000000 | tf_op jit(solution)/shard_map/weight_join/pallas_call | solution.py:126
  (91 shorter events, 7.3 us)
Async XLA Ops:
  0.6 6.5 %copy-start = (bf16[12,192,2,128]{3,2,1,0:T(2,128)(2,1)S(1)}, bf16[12,192,2,128]{3,2,1,0:T(2,128)(2,1)}, u32[]{:S(2)}) copy-start(bf16[12,192,2,128]{3,2,1,0:T(2,128)(2,1)} %high_ref.1) | copy-start | bytes 3538948
  4.4 9.7 %copy-start.5 = (bf16[4,6,128,128]{3,2,1,0:T(8,128)(2,1)S(1)}, bf16[4,6,128,128]{3,2,1,0:T(8,128)(2,1)}, u32[]{:S(2)}) copy-start(bf16[4,6,128,128]{3,2,1,0:T(8,128)(2,1)} %get-tuple-element.41) | copy-start | bytes 2359300
  5.6 12.0 %collective-permute-start.2 = (bf16[12,3,2,2048]{3,2,1,0:T(2,128)(2,1)S(1)}, bf16[12,3,2,2048]{3,2,1,0:T(2,128)(2,1)S(1)}, u32[]{:S(2)}, u32[]{:S(2)}) collective-permute-start(bf16[12,3,2,2048]{3,2,1,0:T(2,128)(2,1)S(1)} %slice.132), channel_id=1, source_target_pairs={{0,15},{1,0},{2,1},{3,2},{4,3},{5,4},{6,5},{7,6},{8,7},{9,8},{10,9... | collective-permute-start | bytes 884744 | tf_op jit(solution)/shard_map/ppermute | solution.py:62
  8.4 23.4 %collective-permute-start.3 = (bf16[6,192,2,128]{3,2,1,0:T(2,128)(2,1)}, bf16[6,192,2,128]{3,2,1,0:T(2,128)(2,1)S(1)}, u32[]{:S(2)}, u32[]{:S(2)}) collective-permute-start(bf16[6,192,2,128]{3,2,1,0:T(2,128)(2,1)} %slice.135), channel_id=1, source_target_pairs={{0,96},{1,97},{2,98},{3,99},{4,100},{5,101},{6,102},{7,103},{8,104... | collective-permute-start | bytes 1769480 | tf_op jit(solution)/shard_map/ppermute | solution.py:49
  14.1 3.5 %slice-start = ((bf16[12,12,2,2048]{3,2,1,0:T(2,128)(2,1)}), bf16[12,9,2,2048]{3,2,1,0:T(2,128)(2,1)S(1)}, s32[]{:S(2)}) async-start(bf16[12,12,2,2048]{3,2,1,0:T(2,128)(2,1)} %param.5), calls=%async_computation | async-start | bytes 1769472 | tf_op jit(solution)/shard_map/slice | solution.py:403
  14.2 8.6 %collective-permute-start = (bf16[2,6,128,128]{3,2,1,0:T(8,128)(2,1)S(1)}, bf16[2,6,128,128]{3,2,1,0:T(8,128)(2,1)S(1)}, u32[]{:S(2)}, u32[]{:S(2)}) collective-permute-start(bf16[2,6,128,128]{3,2,1,0:T(8,128)(2,1)S(1)} %stack.39), channel_id=1, source_target_pairs={{0,8},{1,9},{2,10},{3,11},{4,12},{5,13},{6,14},{7,15},{8,0},{9,1},... | collective-permute-start | bytes 1179656 | tf_op jit(solution)/shard_map/ppermute | solution.py:37
  24.2 14.4 %collective-permute-start.1 = (bf16[2,6,128,128]{3,2,1,0:T(8,128)(2,1)}, bf16[2,6,128,128]{3,2,1,0:T(8,128)(2,1)}, u32[]{:S(2)}, u32[]{:S(2)}) collective-permute-start(bf16[2,6,128,128]{3,2,1,0:T(8,128)(2,1)} %pad_maximum_fusion.5), channel_id=1, source_target_pairs={{0,1},{1,0},{2,3},{3,2},{4,5},{5,4},{6,7},{7,6},{8,9},{9,8},{10,11... | collective-permute-start | bytes 1179656 | tf_op jit(solution)/shard_map/ppermute | solution.py:33
  31.2 0.7 copy-start.1
  31.7 9.8 %copy-start.6 = (bf16[6,128,128]{2,1,0:T(8,128)(2,1)S(1)}, bf16[6,128,128]{2,1,0:T(8,128)(2,1)}, u32[]{:S(2)}) copy-start(bf16[6,128,128]{2,1,0:T(8,128)(2,1)} %get-tuple-element.89) | copy-start | bytes 589828
  31.7 9.7 %copy-start.7 = (bf16[6,128,128]{2,1,0:T(8,128)(2,1)S(1)}, bf16[6,128,128]{2,1,0:T(8,128)(2,1)}, u32[]{:S(2)}) copy-start(bf16[6,128,128]{2,1,0:T(8,128)(2,1)} %get-tuple-element.91) | copy-start | bytes 589828
  31.7 9.7 %copy-start.11 = (bf16[8,128,128]{2,1,0:T(8,128)(2,1)S(1)}, bf16[8,128,128]{2,1,0:T(8,128)(2,1)}, u32[]{:S(2)}) copy-start(bf16[8,128,128]{2,1,0:T(8,128)(2,1)} %get-tuple-element.42) | copy-start | bytes 786436
  32.8 10.1 %collective-permute-start.5 = (bf16[2,2,4,6,6,2,128]{6,5,4,3,2,1,0:T(2,128)(2,1)S(1)}, bf16[2,2,4,6,6,2,128]{6,5,4,3,2,1,0:T(2,128)(2,1)S(1)}, u32[]{:S(2)}, u32[]{:S(2)}) collective-permute-start(bf16[2,2,4,6,6,2,128]{6,5,4,3,2,1,0:T(2,128)(2,1)S(1)} %get-tuple-element.50), channel_id=1, source_target_pairs={{0,2},{1,3},{2,4},{3,5},{4,6},{5,7},{6,0},{7,1},{8,10},{9,11},{10,... | collective-permute-start | bytes 884744 | tf_op jit(solution)/shard_map/ppermute | solution.py:41
  32.8 16.0 %collective-permute-start.6 = (bf16[2,2,4,6,6,2,128]{6,5,4,3,2,1,0:T(2,128)(2,1)S(1)}, bf16[2,2,4,6,6,2,128]{6,5,4,3,2,1,0:T(2,128)(2,1)S(1)}, u32[]{:S(2)}, u32[]{:S(2)}) collective-permute-start(bf16[2,2,4,6,6,2,128]{6,5,4,3,2,1,0:T(2,128)(2,1)S(1)} %get-tuple-element.51), channel_id=1, source_target_pairs={{0,4},{1,5},{2,6},{3,7},{4,0},{5,1},{6,2},{7,3},{8,12},{9,13},{10,... | collective-permute-start | bytes 884744 | tf_op jit(solution)/shard_map/ppermute | solution.py:41
  35.3 14.0 %collective-permute-start.7 = (bf16[2,2,4,6,6,2,128]{6,5,4,3,2,1,0:T(2,128)(2,1)S(1)}, bf16[2,2,4,6,6,2,128]{6,5,4,3,2,1,0:T(2,128)(2,1)S(1)}, u32[]{:S(2)}, u32[]{:S(2)}) collective-permute-start(bf16[2,2,4,6,6,2,128]{6,5,4,3,2,1,0:T(2,128)(2,1)S(1)} %get-tuple-element.52), channel_id=1, source_target_pairs={{0,6},{1,7},{2,0},{3,1},{4,2},{5,3},{6,4},{7,5},{8,14},{9,15},{10,... | collective-permute-start | bytes 884744 | tf_op jit(solution)/shard_map/ppermute | solution.py:41
  36.4 15.9 %collective-permute-start.4 = (bf16[2,72,2048]{2,1,0:T(8,128)(2,1)S(1)}, bf16[2,72,2048]{2,1,0:T(8,128)(2,1)S(1)}, u32[]{:S(2)}, u32[]{:S(2)}) collective-permute-start(bf16[2,72,2048]{2,1,0:T(8,128)(2,1)S(1)} %squeeze.25), channel_id=1, source_target_pairs={{0,96},{1,97},{2,98},{3,99},{4,100},{5,101},{6,102},{7,103},{8,104... | collective-permute-start | bytes 1769480 | tf_op jit(solution)/shard_map/ppermute | solution.py:49
  38.6 14.6 %collective-permute-start.8 = (bf16[2,72,2048]{2,1,0:T(8,128)(2,1)S(1)}, bf16[2,72,2048]{2,1,0:T(8,128)(2,1)S(1)}, u32[]{:S(2)}, u32[]{:S(2)}) collective-permute-start(bf16[2,72,2048]{2,1,0:T(8,128)(2,1)S(1)} %squeeze.26), channel_id=1, source_target_pairs={{0,8},{1,9},{2,10},{3,11},{4,12},{5,13},{6,14},{7,15},{8,0},{9,1},... | collective-permute-start | bytes 1769480 | tf_op jit(solution)/shard_map/ppermute | solution.py:37
  53.2 22.3 %collective-permute-start.12 = (bf16[32,128,128]{2,1,0:T(8,128)(2,1)S(1)}, bf16[32,128,128]{2,1,0:T(8,128)(2,1)S(1)}, u32[]{:S(2)}, u32[]{:S(2)}) collective-permute-start(bf16[32,128,128]{2,1,0:T(8,128)(2,1)S(1)} %pad_maximum_fusion.2.refs_12_), channel_id=1, source_target_pairs={{0,6},{1,7},{2,0},{3,1},{4,2},{5,3},{6,4},{7,5},{8,14},{9,15},{10,... | collective-permute-start | bytes 3145736 | tf_op jit(solution)/shard_map/ppermute | solution.py:41
  54.8 12.9 %collective-permute-start.14 = (bf16[2,72,2048]{2,1,0:T(8,128)(2,1)S(1)}, bf16[2,72,2048]{2,1,0:T(8,128)(2,1)S(1)}, u32[]{:S(2)}, u32[]{:S(2)}) collective-permute-start(bf16[2,72,2048]{2,1,0:T(8,128)(2,1)S(1)} %collective-permute-done.4), channel_id=1, source_target_pairs={{0,16},{1,17},{2,18},{3,19},{4,20},{5,21},{6,22},{7,23},{8,24},{9,... | collective-permute-start | bytes 1769480 | tf_op jit(solution)/shard_map/ppermute | solution.py:58
  54.8 24.1 %collective-permute-start.11 = (bf16[32,128,128]{2,1,0:T(8,128)(2,1)S(1)}, bf16[32,128,128]{2,1,0:T(8,128)(2,1)S(1)}, u32[]{:S(2)}, u32[]{:S(2)}) collective-permute-start(bf16[32,128,128]{2,1,0:T(8,128)(2,1)S(1)} %pad_maximum_fusion.2.refs_12_), channel_id=1, source_target_pairs={{0,2},{1,3},{2,4},{3,5},{4,6},{5,7},{6,0},{7,1},{8,10},{9,11},{10,... | collective-permute-start | bytes 3145736 | tf_op jit(solution)/shard_map/ppermute | solution.py:41
  54.8 24.1 %collective-permute-start.13 = (bf16[2,72,2048]{2,1,0:T(8,128)(2,1)S(1)}, bf16[2,72,2048]{2,1,0:T(8,128)(2,1)S(1)}, u32[]{:S(2)}, u32[]{:S(2)}) collective-permute-start(bf16[2,72,2048]{2,1,0:T(8,128)(2,1)S(1)} %collective-permute-done.4), channel_id=1, source_target_pairs={{0,24},{1,25},{2,26},{3,27},{4,28},{5,29},{6,30},{7,31},{8,16},{9,... | collective-permute-start | bytes 1769480 | tf_op jit(solution)/shard_map/ppermute | solution.py:58
  57.9 23.4 %collective-permute-start.10 = (bf16[4,2,4,72,128]{4,3,2,1,0:T(8,128)(2,1)S(1)}, bf16[4,2,4,72,128]{4,3,2,1,0:T(8,128)(2,1)S(1)}, u32[]{:S(2)}, u32[]{:S(2)}) collective-permute-start(bf16[4,2,4,72,128]{4,3,2,1,0:T(8,128)(2,1)S(1)} %bitcast.43), channel_id=1, source_target_pairs={{0,8},{1,9},{2,10},{3,11},{4,12},{5,13},{6,14},{7,15},{8,0},{9,1},... | collective-permute-start | bytes 1769480 | tf_op jit(solution)/shard_map/ppermute | solution.py:37
  67.7 17.8 %copy-start.9 = (bf16[2,144,2048]{2,1,0:T(8,128)(2,1)}, bf16[2,144,2048]{2,1,0:T(8,128)(2,1)S(1)}, u32[]{:S(2)}) copy-start(bf16[2,144,2048]{2,1,0:T(8,128)(2,1)S(1)} %constant_dynamic-update-slice_fusion.2.refs_8_) | copy-start | bytes 3538948
  67.7 26.1 %collective-permute-start.19 = (bf16[2,144,2048]{2,1,0:T(8,128)(2,1)S(1)}, bf16[2,144,2048]{2,1,0:T(8,128)(2,1)S(1)}, u32[]{:S(2)}, u32[]{:S(2)}) collective-permute-start(bf16[2,144,2048]{2,1,0:T(8,128)(2,1)S(1)} %constant_dynamic-update-slice_fusion.2.refs_8_), channel_id=1, source_target_pairs={{0,1},{1,0},{2,3},{3,2},{4,5},{5,4},{6,7},{7,6},{8,9},{9,8},{10,11... | collective-permute-start | bytes 3538952 | tf_op jit(solution)/shard_map/ppermute | solution.py:33
  75.5 7.2 %collective-permute-start.9 = (bf16[4,2,4,72,128]{4,3,2,1,0:T(8,128)(2,1)S(1)}, bf16[4,2,4,72,128]{4,3,2,1,0:T(8,128)(2,1)S(1)}, u32[]{:S(2)}, u32[]{:S(2)}) collective-permute-start(bf16[4,2,4,72,128]{4,3,2,1,0:T(8,128)(2,1)S(1)} %bitcast.44), channel_id=1, source_target_pairs={{0,1},{1,0},{2,3},{3,2},{4,5},{5,4},{6,7},{7,6},{8,9},{9,8},{10,11... | collective-permute-start | bytes 1769480 | tf_op jit(solution)/shard_map/ppermute | solution.py:33
  81.3 12.5 %collective-permute-start.16 = (bf16[4,2,4,72,128]{4,3,2,1,0:T(8,128)(2,1)S(1)}, bf16[4,2,4,72,128]{4,3,2,1,0:T(8,128)(2,1)S(1)}, u32[]{:S(2)}, u32[]{:S(2)}) collective-permute-start(bf16[4,2,4,72,128]{4,3,2,1,0:T(8,128)(2,1)S(1)} %bitcast.53), channel_id=1, source_target_pairs={{0,24},{1,25},{2,26},{3,27},{4,28},{5,29},{6,30},{7,31},{8,16},{9,... | collective-permute-start | bytes 1769480 | tf_op jit(solution)/shard_map/ppermute | solution.py:58
  82.7 11.1 %collective-permute-start.15 = (bf16[4,2,4,72,128]{4,3,2,1,0:T(8,128)(2,1)S(1)}, bf16[4,2,4,72,128]{4,3,2,1,0:T(8,128)(2,1)S(1)}, u32[]{:S(2)}, u32[]{:S(2)}) collective-permute-start(bf16[4,2,4,72,128]{4,3,2,1,0:T(8,128)(2,1)S(1)} %bitcast.54), channel_id=1, source_target_pairs={{0,16},{1,17},{2,18},{3,19},{4,20},{5,21},{6,22},{7,23},{8,24},{9,... | collective-permute-start | bytes 1769480 | tf_op jit(solution)/shard_map/ppermute | solution.py:58
  82.7 9.5 %collective-permute-start.17 = (bf16[16,128,128]{2,1,0:T(8,128)(2,1)S(1)}, bf16[16,128,128]{2,1,0:T(8,128)(2,1)S(1)}, u32[]{:S(2)}, u32[]{:S(2)}) collective-permute-start(bf16[16,128,128]{2,1,0:T(8,128)(2,1)S(1)} %slice.176), channel_id=1, source_target_pairs={{0,2},{1,3},{2,4},{3,5},{4,6},{5,7},{6,0},{7,1},{8,10},{9,11},{10,... | collective-permute-start | bytes 1572872 | tf_op jit(solution)/shard_map/ppermute | solution.py:41
  82.7 9.5 %collective-permute-start.18 = (bf16[16,128,128]{2,1,0:T(8,128)(2,1)S(1)}, bf16[16,128,128]{2,1,0:T(8,128)(2,1)S(1)}, u32[]{:S(2)}, u32[]{:S(2)}) collective-permute-start(bf16[16,128,128]{2,1,0:T(8,128)(2,1)S(1)} %slice.177), channel_id=1, source_target_pairs={{0,6},{1,7},{2,0},{3,1},{4,2},{5,3},{6,4},{7,5},{8,14},{9,15},{10,... | collective-permute-start | bytes 1572872 | tf_op jit(solution)/shard_map/ppermute | solution.py:41
  85.5 20.4 %copy-start.10 = (bf16[2,144,2048]{2,1,0:T(8,128)(2,1)}, bf16[2,144,2048]{2,1,0:T(8,128)(2,1)S(1)}, u32[]{:S(2)}) copy-start(bf16[2,144,2048]{2,1,0:T(8,128)(2,1)S(1)} %constant_dynamic-update-slice_fusion.refs_10_) | copy-start | bytes 3538948
  93.8 12.1 %copy-start.12 = (bf16[2,144,2048]{2,1,0:T(8,128)(2,1)}, bf16[2,144,2048]{2,1,0:T(8,128)(2,1)S(1)}, u32[]{:S(2)}) copy-start(bf16[2,144,2048]{2,1,0:T(8,128)(2,1)S(1)} %collective-permute-done.19.refs_9_) | copy-start | bytes 3538948
  93.8 12.1 %collective-permute-start.23 = (bf16[2,144,2048]{2,1,0:T(8,128)(2,1)S(1)}, bf16[2,144,2048]{2,1,0:T(8,128)(2,1)S(1)}, u32[]{:S(2)}, u32[]{:S(2)}) collective-permute-start(bf16[2,144,2048]{2,1,0:T(8,128)(2,1)S(1)} %constant_dynamic-update-slice_fusion.refs_10_), channel_id=1, source_target_pairs={{0,1},{1,0},{2,3},{3,2},{4,5},{5,4},{6,7},{7,6},{8,9},{9,8},{10,11... | collective-permute-start | bytes 3538952 | tf_op jit(solution)/shard_map/ppermute | solution.py:33
  100.9 3.3 %collective-permute-start.20 = (bf16[4,2,4,72,128]{4,3,2,1,0:T(8,128)(2,1)S(1)}, bf16[4,2,4,72,128]{4,3,2,1,0:T(8,128)(2,1)S(1)}, u32[]{:S(2)}, u32[]{:S(2)}) collective-permute-start(bf16[4,2,4,72,128]{4,3,2,1,0:T(8,128)(2,1)S(1)} %collective-permute-done.10.refs_2_), channel_id=1, source_target_pairs={{0,1},{1,0},{2,3},{3,2},{4,5},{5,4},{6,7},{7,6},{8,9},{9,8},{10,11... | collective-permute-start | bytes 1769480 | tf_op jit(solution)/shard_map/ppermute | solution.py:33
  101.0 4.1 %collective-permute-start.21 = (bf16[4,2,4,72,128]{4,3,2,1,0:T(8,128)(2,1)S(1)}, bf16[4,2,4,72,128]{4,3,2,1,0:T(8,128)(2,1)S(1)}, u32[]{:S(2)}, u32[]{:S(2)}) collective-permute-start(bf16[4,2,4,72,128]{4,3,2,1,0:T(8,128)(2,1)S(1)} %collective-permute-done.15.refs_4_), channel_id=1, source_target_pairs={{0,1},{1,0},{2,3},{3,2},{4,5},{5,4},{6,7},{7,6},{8,9},{9,8},{10,11... | collective-permute-start | bytes 1769480 | tf_op jit(solution)/shard_map/ppermute | solution.py:33
  101.4 4.5 %collective-permute-start.22 = (bf16[4,2,4,72,128]{4,3,2,1,0:T(8,128)(2,1)S(1)}, bf16[4,2,4,72,128]{4,3,2,1,0:T(8,128)(2,1)S(1)}, u32[]{:S(2)}, u32[]{:S(2)}) collective-permute-start(bf16[4,2,4,72,128]{4,3,2,1,0:T(8,128)(2,1)S(1)} %collective-permute-done.16.refs_6_), channel_id=1, source_target_pairs={{0,1},{1,0},{2,3},{3,2},{4,5},{5,4},{6,7},{7,6},{8,9},{9,8},{10,11... | collective-permute-start | bytes 1769480 | tf_op jit(solution)/shard_map/ppermute | solution.py:33
  105.9 1.1 copy-start.13
  135.9 4.7 %collective-permute-start.24 = (bf16[2,4,2,4,144,128]{5,4,3,2,1,0:T(8,128)(2,1)}, bf16[2,4,2,4,144,128]{5,4,3,2,1,0:T(8,128)(2,1)S(1)}, u32[]{:S(2)}, u32[]{:S(2)}) collective-permute-start(bf16[2,4,2,4,144,128]{5,4,3,2,1,0:T(8,128)(2,1)} %get-tuple-element.66), channel_id=1, source_target_pairs={{0,1},{1,0},{2,3},{3,2},{4,5},{5,4},{6,7},{7,6},{8,9},{9,8},{10,11... | collective-permute-start | bytes 7077896 | tf_op jit(solution)/shard_map/ppermute | solution.py:33
  136.2 24.5 %collective-permute-start.32 = (bf16[32,128,128]{2,1,0:T(8,128)(2,1)S(1)}, bf16[32,128,128]{2,1,0:T(8,128)(2,1)S(1)}, u32[]{:S(2)}, u32[]{:S(2)}) collective-permute-start(bf16[32,128,128]{2,1,0:T(8,128)(2,1)S(1)} %get-tuple-element.72), channel_id=1, source_target_pairs={{0,6},{1,7},{2,0},{3,1},{4,2},{5,3},{6,4},{7,5},{8,14},{9,15},{10,... | collective-permute-start | bytes 3145736 | tf_op jit(solution)/shard_map/ppermute | solution.py:41
  137.7 25.5 %collective-permute-start.33 = (bf16[32,128,128]{2,1,0:T(8,128)(2,1)S(1)}, bf16[32,128,128]{2,1,0:T(8,128)(2,1)S(1)}, u32[]{:S(2)}, u32[]{:S(2)}) collective-permute-start(bf16[32,128,128]{2,1,0:T(8,128)(2,1)S(1)} %get-tuple-element.74), channel_id=1, source_target_pairs={{0,2},{1,3},{2,4},{3,5},{4,6},{5,7},{6,0},{7,1},{8,10},{9,11},{10,... | collective-permute-start | bytes 3145736 | tf_op jit(solution)/shard_map/ppermute | solution.py:41
  142.6 20.7 %collective-permute-start.25 = (bf16[4,2,4,72,128]{4,3,2,1,0:T(8,128)(2,1)S(1)}, bf16[4,2,4,72,128]{4,3,2,1,0:T(8,128)(2,1)S(1)}, u32[]{:S(2)}, u32[]{:S(2)}) collective-permute-start(bf16[4,2,4,72,128]{4,3,2,1,0:T(8,128)(2,1)S(1)} %slice.243), channel_id=1, source_target_pairs={{0,16},{1,17},{2,18},{3,19},{4,20},{5,21},{6,22},{7,23},{8,24},{9,... | collective-permute-start | bytes 1769480 | tf_op jit(solution)/shard_map/ppermute | solution.py:58
  144.5 18.8 %collective-permute-start.26 = (bf16[4,2,4,72,128]{4,3,2,1,0:T(8,128)(2,1)S(1)}, bf16[4,2,4,72,128]{4,3,2,1,0:T(8,128)(2,1)S(1)}, u32[]{:S(2)}, u32[]{:S(2)}) collective-permute-start(bf16[4,2,4,72,128]{4,3,2,1,0:T(8,128)(2,1)S(1)} %get-tuple-element.85), channel_id=1, source_target_pairs={{0,24},{1,25},{2,26},{3,27},{4,28},{5,29},{6,30},{7,31},{8,16},{9,... | collective-permute-start | bytes 1769480 | tf_op jit(solution)/shard_map/ppermute | solution.py:58
  160.7 10.0 %copy-start.3 = (bf16[32,128,128]{2,1,0:T(8,128)(2,1)}, bf16[32,128,128]{2,1,0:T(8,128)(2,1)S(1)}, u32[]{:S(2)}) copy-start(bf16[32,128,128]{2,1,0:T(8,128)(2,1)S(1)} %collective-permute-done.32) | copy-start | bytes 3145732
  163.5 12.2 %collective-permute-start.34 = (bf16[16,128,128]{2,1,0:T(8,128)(2,1)S(1)}, bf16[16,128,128]{2,1,0:T(8,128)(2,1)S(1)}, u32[]{:S(2)}, u32[]{:S(2)}) collective-permute-start(bf16[16,128,128]{2,1,0:T(8,128)(2,1)S(1)} %add_convert_fusion.2), channel_id=1, source_target_pairs={{0,6},{1,7},{2,0},{3,1},{4,2},{5,3},{6,4},{7,5},{8,14},{9,15},{10,... | collective-permute-start | bytes 1572872 | tf_op jit(solution)/shard_map/ppermute | solution.py:41
  164.0 13.3 %collective-permute-start.35 = (bf16[16,128,128]{2,1,0:T(8,128)(2,1)S(1)}, bf16[16,128,128]{2,1,0:T(8,128)(2,1)S(1)}, u32[]{:S(2)}, u32[]{:S(2)}) collective-permute-start(bf16[16,128,128]{2,1,0:T(8,128)(2,1)S(1)} %add_convert_fusion.1), channel_id=1, source_target_pairs={{0,2},{1,3},{2,4},{3,5},{4,6},{5,7},{6,0},{7,1},{8,10},{9,11},{10,... | collective-permute-start | bytes 1572872 | tf_op jit(solution)/shard_map/ppermute | solution.py:41
  165.0 14.4 %collective-permute-start.27 = (bf16[4,2,4,72,128]{4,3,2,1,0:T(8,128)(2,1)S(1)}, bf16[4,2,4,72,128]{4,3,2,1,0:T(8,128)(2,1)S(1)}, u32[]{:S(2)}, u32[]{:S(2)}) collective-permute-start(bf16[4,2,4,72,128]{4,3,2,1,0:T(8,128)(2,1)S(1)} %get-tuple-element.68), channel_id=1, source_target_pairs={{0,8},{1,9},{2,10},{3,11},{4,12},{5,13},{6,14},{7,15},{8,0},{9,1},... | collective-permute-start | bytes 1769480 | tf_op jit(solution)/shard_map/ppermute | solution.py:37
  166.2 15.8 %collective-permute-start.28 = (bf16[4,2,4,72,128]{4,3,2,1,0:T(8,128)(2,1)S(1)}, bf16[4,2,4,72,128]{4,3,2,1,0:T(8,128)(2,1)S(1)}, u32[]{:S(2)}, u32[]{:S(2)}) collective-permute-start(bf16[4,2,4,72,128]{4,3,2,1,0:T(8,128)(2,1)S(1)} %add_convert_fusion), channel_id=1, source_target_pairs={{0,32},{1,33},{2,34},{3,35},{4,36},{5,37},{6,38},{7,39},{8,40},{9,... | collective-permute-start | bytes 1769480 | tf_op jit(solution)/shard_map/ppermute | solution.py:49
  170.7 6.7 %slice-start.1 = ((bf16[32,128,128]{2,1,0:T(8,128)(2,1)}), bf16[16,128,128]{2,1,0:T(8,128)(2,1)S(1)}, s32[]{:S(2)}) async-start(bf16[32,128,128]{2,1,0:T(8,128)(2,1)} %copy-done.3), calls=%async_computation.1 | async-start | bytes 1048576 | tf_op jit(solution)/shard_map/slice | solution.py:452
  177.9 21.9 %copy-start.2 = (f32[32,128,128]{2,1,0:T(8,128)}, f32[32,128,128]{2,1,0:T(8,128)S(1)}, u32[]{:S(2)}) copy-start(f32[32,128,128]{2,1,0:T(8,128)S(1)} %convert_add_fusion.2.a_ref) | copy-start | bytes 6291460
  178.1 17.6 %collective-permute-start.36 = (bf16[2,6,128,128]{3,2,1,0:T(8,128)(2,1)S(1)}, bf16[2,6,128,128]{3,2,1,0:T(8,128)(2,1)S(1)}, u32[]{:S(2)}, u32[]{:S(2)}) collective-permute-start(bf16[2,6,128,128]{3,2,1,0:T(8,128)(2,1)S(1)} %bitcast.55), channel_id=1, source_target_pairs={{0,8},{1,9},{2,10},{3,11},{4,12},{5,13},{6,14},{7,15},{8,0},{9,1},... | collective-permute-start | bytes 1179656 | tf_op jit(solution)/shard_map/ppermute | solution.py:37
  182.1 7.1 %collective-permute-start.31 = (bf16[2,4,144,128]{3,2,1,0:T(8,128)(2,1)S(1)}, bf16[2,4,144,128]{3,2,1,0:T(8,128)(2,1)S(1)}, u32[]{:S(2)}, u32[]{:S(2)}) collective-permute-start(bf16[2,4,144,128]{3,2,1,0:T(8,128)(2,1)S(1)} %get-tuple-element.81), channel_id=1, source_target_pairs={{0,2},{1,3},{2,4},{3,5},{4,6},{5,7},{6,0},{7,1},{8,10},{9,11},{10,... | collective-permute-start | bytes 884744 | tf_op jit(solution)/shard_map/ppermute | solution.py:41
  182.4 8.1 %collective-permute-start.29 = (bf16[2,4,144,128]{3,2,1,0:T(8,128)(2,1)S(1)}, bf16[2,4,144,128]{3,2,1,0:T(8,128)(2,1)S(1)}, u32[]{:S(2)}, u32[]{:S(2)}) collective-permute-start(bf16[2,4,144,128]{3,2,1,0:T(8,128)(2,1)S(1)} %get-tuple-element.82), channel_id=1, source_target_pairs={{0,6},{1,7},{2,0},{3,1},{4,2},{5,3},{6,4},{7,5},{8,14},{9,15},{10,... | collective-permute-start | bytes 884744 | tf_op jit(solution)/shard_map/ppermute | solution.py:41
  184.8 10.8 %collective-permute-start.30 = (bf16[2,4,144,128]{3,2,1,0:T(8,128)(2,1)S(1)}, bf16[2,4,144,128]{3,2,1,0:T(8,128)(2,1)S(1)}, u32[]{:S(2)}, u32[]{:S(2)}) collective-permute-start(bf16[2,4,144,128]{3,2,1,0:T(8,128)(2,1)S(1)} %get-tuple-element.83), channel_id=1, source_target_pairs={{0,4},{1,5},{2,6},{3,7},{4,0},{5,1},{6,2},{7,3},{8,12},{9,13},{10,... | collective-permute-start | bytes 884744 | tf_op jit(solution)/shard_map/ppermute | solution.py:41
  195.6 4.6 %copy-start.4 = (bf16[2,6,128,128]{3,2,1,0:T(8,128)(2,1)}, bf16[2,6,128,128]{3,2,1,0:T(8,128)(2,1)S(1)}, u32[]{:S(2)}) copy-start(bf16[2,6,128,128]{3,2,1,0:T(8,128)(2,1)S(1)} %collective-permute-done.36.c_ref) | copy-start | bytes 1179652
  195.7 7.6 %collective-permute-start.37 = (bf16[2,6,128,128]{3,2,1,0:T(8,128)(2,1)S(1)}, bf16[2,6,128,128]{3,2,1,0:T(8,128)(2,1)S(1)}, u32[]{:S(2)}, u32[]{:S(2)}) collective-permute-start(bf16[2,6,128,128]{3,2,1,0:T(8,128)(2,1)S(1)} %pad_maximum_fusion.6), channel_id=1, source_target_pairs={{0,1},{1,0},{2,3},{3,2},{4,5},{5,4},{6,7},{7,6},{8,9},{9,8},{10,11... | collective-permute-start | bytes 1179656 | tf_op jit(solution)/shard_map/ppermute | solution.py:33
  203.3 0.7 copy-start.8
where the time goes:
time: 208 us
  waiting for transfers between devices  77.9 us (37%)
  starting transfers between devices  69.5 us (33%)
  Pallas kernels  38.3 us (18%)
  local copies, waits for them, and re-layouts  11.3 us (5%)
  other arithmetic  9.45 us (5%)
    ppermute x14, waiting for transfers between devices, shift_y(): lax.ppermute(value, 'lon', [(lon_of(x, y, c), lon_of(x, (y + by) % NY, c)...  50.6 us
    pallas_call x1, Pallas kernels, window_pass(): pl.pallas_call(window_kernel, grid_spec=pltpu.PrefetchScalarGridSpec(num_...  28.9 us
    ppermute x9, starting transfers between devices, swap_c(): lax.ppermute(value, 'lon', [(lon_of(x, y, c), lon_of(x, y, 1 - c)) for x,...  26.9 us
    ppermute x14, starting transfers between devices, shift_y(): lax.ppermute(value, 'lon', [(lon_of(x, y, c), lon_of(x, (y + by) % NY, c)...  14.1 us
    ppermute x3, starting transfers between devices, hop_z(): return lax.ppermute(value, ('lat', 'lon'), pairs)  12.2 us
    ppermute x6, waiting for transfers between devices, across(): return lax.ppermute(value, ('lat', 'lon'), pairs)  11 us
    ppermute x5, starting transfers between devices, swap_x(): lax.ppermute(value, 'lon', [(lon_of(x, y, c), lon_of(1 - x, y, c)) for x,...  8.41 us
    ppermute x9, waiting for transfers between devices, swap_c(): lax.ppermute(value, 'lon', [(lon_of(x, y, c), lon_of(x, y, 1 - c)) for x,...  7.38 us
  transfers between devices with their start and end apart: 38, of which 24 were waited for; matrix products, arithmetic and copies ran while one was open for 8% of the time, Pallas kernels for 1%

commit v1 on v0

--- a/solution.py
+++ b/solution.py
@@ -377,7 +377,7 @@
             ],
         ),
         out_shape=part_shapes + [shape((n, 128, 128), t) for n, t in zip(sizes, dtypes)],
-        compiler_params=pltpu.CompilerParams(vmem_limit_bytes=40 * MIB),
+        compiler_params=pltpu.CompilerParams(vmem_limit_bytes=30 * MIB),
         cost_estimate=pl.CostEstimate(flops=32 * 10**9, bytes_accessed=30 * 10**6, transcendentals=10**6),
         name="window_pass",
     )(scalars, *xs, *us, *ws)

time: 208 us -> 205 us (0.986)
  Pallas kernels: 38.3 us -> 36.1 us
    pallas_call x1, Pallas kernels: 28.9 us -> 26.7 us  [window_pass(): pl.pallas_call(window_kernel, grid_spec=pltpu.PrefetchScalarGridSpec(num_...]
where the time goes in v1:
time: 205 us; the launch traced here: 204 us
  waiting for transfers between devices  78.8 us (38%)
  starting transfers between devices  69.8 us (34%)
  Pallas kernels  36.1 us (18%)
  local copies, waits for them, and re-layouts  10.3 us (5%)
  other arithmetic  8.13 us (4%)
    ppermute x14, waiting for transfers between devices, shift_y(): lax.ppermute(value, 'lon', [(lon_of(x, y, c), lon_of(x, (y + by) % NY, c)...  51.9 us
    ppermute x9, starting transfers between devices, swap_c(): lax.ppermute(value, 'lon', [(lon_of(x, y, c), lon_of(x, y, 1 - c)) for x,...  27.1 us
    pallas_call x1, Pallas kernels, window_pass(): pl.pallas_call(window_kernel, grid_spec=pltpu.PrefetchScalarGridSpec(num_...  26.7 us
    ppermute x14, starting transfers between devices, shift_y(): lax.ppermute(value, 'lon', [(lon_of(x, y, c), lon_of(x, (y + by) % NY, c)...  14.1 us
    ppermute x3, starting transfers between devices, hop_z(): return lax.ppermute(value, ('lat', 'lon'), pairs)  12.3 us
    ppermute x6, waiting for transfers between devices, across(): return lax.ppermute(value, ('lat', 'lon'), pairs)  10.9 us
    ppermute x5, starting transfers between devices, swap_x(): lax.ppermute(value, 'lon', [(lon_of(x, y, c), lon_of(1 - x, y, c)) for x,...  8.4 us
    ppermute x9, waiting for transfers between devices, swap_c(): lax.ppermute(value, 'lon', [(lon_of(x, y, c), lon_of(x, y, 1 - c)) for x,...  7.19 us
  transfers between devices with their start and end apart: 38, of which 24 were waited for; matrix products, arithmetic and copies ran while one was open for 8% of the time, Pallas kernels for 1%

profile of v1, /device:TPU:1, one launch (start us, length us, event | category | flops | bytes accessed | tf_op | source)
XLA Modules:
  0.0 204.3 jit_solution(1686950447464228643)
XLA Ops:
  0.7 0.6 pad_add_fusion.s_ref
  1.3 3.1 %weight_split.1 = (bf16[4,6,128,128]{3,2,1,0:T(8,128)(2,1)}, bf16[8,128,128]{2,1,0:T(8,128)(2,1)}) custom-call(s32[4]{0:T(128)} %pad_add_fusion.s_ref, bf16[128,3072]{1,0:T(8,128)(2,1)} %q_ref.1, bf16[64,2048]{1,0:T(8,128)(2,1)} %o_ref.1), custom_call_target="tpu_custom_call" | custom-call | bytes 2000000 | tf_op jit(solution)/shard_map/weight_split/pallas_call | solution.py:93
  4.4 1.2 slice.132
  5.6 1.5 collective-permute-start.2
  7.1 1.2 slice.135
  8.3 5.7 %collective-permute-start.3 = (bf16[6,192,2,128]{3,2,1,0:T(2,128)(2,1)}, bf16[6,192,2,128]{3,2,1,0:T(2,128)(2,1)S(1)}, u32[]{:S(2)}, u32[]{:S(2)}) collective-permute-start(bf16[6,192,2,128]{3,2,1,0:T(2,128)(2,1)} %slice.135), channel_id=1, source_target_pairs={{0,96},{1,97},{2,98},{3,99},{4,100},{5,101},{6,102},{7,103},{8,104... | collective-permute-start | bytes 1769480 | tf_op jit(solution)/shard_map/ppermute | solution.py:49
  14.1 2.8 %collective-permute-start = (bf16[2,6,128,128]{3,2,1,0:T(8,128)(2,1)S(1)}, bf16[2,6,128,128]{3,2,1,0:T(8,128)(2,1)S(1)}, u32[]{:S(2)}, u32[]{:S(2)}) collective-permute-start(bf16[2,6,128,128]{3,2,1,0:T(8,128)(2,1)S(1)} %stack.39), channel_id=1, source_target_pairs={{0,8},{1,9},{2,10},{3,11},{4,12},{5,13},{6,14},{7,15},{8,0},{9,1},... | collective-permute-start | bytes 1179656 | tf_op jit(solution)/shard_map/ppermute | solution.py:37
  17.0 0.7 slice_bitcast_fusion.4
  17.7 1.5 pad_maximum_fusion.1
  19.2 1.0 copy.10
  20.2 2.5 %collective-permute-done = bf16[2,6,128,128]{3,2,1,0:T(8,128)(2,1)S(1)} collective-permute-done((bf16[2,6,128,128]{3,2,1,0:T(8,128)(2,1)S(1)}, bf16[2,6,128,128]{3,2,1,0:T(8,128)(2,1)S(1)}, u32[]{:S(2)}, u32[]{:S(2)}) %collective-permute-start) | collective-permute-done | bytes 393248 | tf_op jit(solution)/shard_map/ppermute | solution.py:37
  22.7 0.7 slice_bitcast_fusion.3
  23.4 0.8 pad_maximum_fusion.5
  24.2 6.0 %collective-permute-start.1 = (bf16[2,6,128,128]{3,2,1,0:T(8,128)(2,1)}, bf16[2,6,128,128]{3,2,1,0:T(8,128)(2,1)}, u32[]{:S(2)}, u32[]{:S(2)}) collective-permute-start(bf16[2,6,128,128]{3,2,1,0:T(8,128)(2,1)} %pad_maximum_fusion.5), channel_id=1, source_target_pairs={{0,1},{1,0},{2,3},{3,2},{4,5},{5,4},{6,7},{7,6},{8,9},{9,8},{10,11... | collective-permute-start | bytes 1179656 | tf_op jit(solution)/shard_map/ppermute | solution.py:33
  30.2 1.0 fusion.10
  31.8 0.9 token_split.1
  32.8 2.5 %collective-permute-start.6 = (bf16[2,2,4,6,6,2,128]{6,5,4,3,2,1,0:T(2,128)(2,1)S(1)}, bf16[2,2,4,6,6,2,128]{6,5,4,3,2,1,0:T(2,128)(2,1)S(1)}, u32[]{:S(2)}, u32[]{:S(2)}) collective-permute-start(bf16[2,2,4,6,6,2,128]{6,5,4,3,2,1,0:T(2,128)(2,1)S(1)} %get-tuple-element.51), channel_id=1, source_target_pairs={{0,4},{1,5},{2,6},{3,7},{4,0},{5,1},{6,2},{7,3},{8,12},{9,13},{10,... | collective-permute-start | bytes 884744 | tf_op jit(solution)/shard_map/ppermute | solution.py:41
  35.2 1.1 collective-permute-start.7
  36.3 2.0 collective-permute-start.4
  38.6 2.8 %collective-permute-start.8 = (bf16[2,72,2048]{2,1,0:T(8,128)(2,1)S(1)}, bf16[2,72,2048]{2,1,0:T(8,128)(2,1)S(1)}, u32[]{:S(2)}, u32[]{:S(2)}) collective-permute-start(bf16[2,72,2048]{2,1,0:T(8,128)(2,1)S(1)} %squeeze.26), channel_id=1, source_target_pairs={{0,8},{1,9},{2,10},{3,11},{4,12},{5,13},{6,14},{7,15},{8,0},{9,1},... | collective-permute-start | bytes 1769480 | tf_op jit(solution)/shard_map/ppermute | solution.py:37
  41.4 1.1 pad_maximum_fusion.2.refs_12_
  43.0 5.8 %collective-permute-done.6 = bf16[2,2,4,6,6,2,128]{6,5,4,3,2,1,0:T(2,128)(2,1)S(1)} collective-permute-done((bf16[2,2,4,6,6,2,128]{6,5,4,3,2,1,0:T(2,128)(2,1)S(1)}, bf16[2,2,4,6,6,2,128]{6,5,4,3,2,1,0:T(2,128)(2,1)S(1)}, u32[]{:S(2)}, u32[]{:S(2)}) %collective-permute-start.6) | collective-permute-done | bytes 294944 | tf_op jit(solution)/shard_map/ppermute | solution.py:41
  49.4 2.2 %pad_maximum_fusion.3 = (bf16[4,2,4,6,6,2,128]{6,5,4,3,2,1,0:T(2,128)(2,1)S(1)}, bf16[4,2,4,6,6,2,128]{6,5,4,3,2,1,0:T(2,128)(2,1)S(1)}) fusion(bf16[1,2,4,6,6,2,128]{6,5,4,3,2,1,0:T(2,128)(2,1)S(1)} %get-tuple-element.100, bf16[1,2,4,6,6,2,128]{6,5,4,3,2,1,0:T(2,128)(2,1)S(1)} %get-tuple-element.98, ...), kind=kLoop, calls=%fused_computation.24 | loop fusion | flops 1769472 | bytes 2359296 | tf_op jit(solution)/shard_map/stack | solution.py:411
  51.6 0.6 collective-permute-done.4
  52.2 0.9 collective-permute-done.8
  53.1 1.6 collective-permute-start.12
  54.7 3.0 %collective-permute-start.13 = (bf16[2,72,2048]{2,1,0:T(8,128)(2,1)S(1)}, bf16[2,72,2048]{2,1,0:T(8,128)(2,1)S(1)}, u32[]{:S(2)}, u32[]{:S(2)}) collective-permute-start(bf16[2,72,2048]{2,1,0:T(8,128)(2,1)S(1)} %collective-permute-done.4), channel_id=1, source_target_pairs={{0,24},{1,25},{2,26},{3,27},{4,28},{5,29},{6,30},{7,31},{8,16},{9,... | collective-permute-start | bytes 1769480 | tf_op jit(solution)/shard_map/ppermute | solution.py:58
  58.1 9.5 %collective-permute-done.14 = bf16[2,72,2048]{2,1,0:T(8,128)(2,1)S(1)} collective-permute-done((bf16[2,72,2048]{2,1,0:T(8,128)(2,1)S(1)}, bf16[2,72,2048]{2,1,0:T(8,128)(2,1)S(1)}, u32[]{:S(2)}, u32[]{:S(2)}) %collective-permute-start.14) | collective-permute-done | bytes 589856 | tf_op jit(solution)/shard_map/ppermute | solution.py:58
  67.6 5.6 %collective-permute-start.19 = (bf16[2,144,2048]{2,1,0:T(8,128)(2,1)S(1)}, bf16[2,144,2048]{2,1,0:T(8,128)(2,1)S(1)}, u32[]{:S(2)}, u32[]{:S(2)}) collective-permute-start(bf16[2,144,2048]{2,1,0:T(8,128)(2,1)S(1)} %constant_dynamic-update-slice_fusion.2.refs_8_), channel_id=1, source_target_pairs={{0,1},{1,0},{2,3},{3,2},{4,5},{5,4},{6,7},{7,6},{8,9},{9,8},{10,11... | collective-permute-start | bytes 3538952 | tf_op jit(solution)/shard_map/ppermute | solution.py:33
  73.2 2.2 %collective-permute-done.12.refs_15_ = bf16[32,128,128]{2,1,0:T(8,128)(2,1)S(1)} collective-permute-done((bf16[32,128,128]{2,1,0:T(8,128)(2,1)S(1)}, bf16[32,128,128]{2,1,0:T(8,128)(2,1)S(1)}, u32[]{:S(2)}, u32[]{:S(2)}) %collective-permute-start.12) | collective-permute-done | bytes 1048608 | tf_op jit(solution)/shard_map/ppermute | solution.py:41
  75.5 3.2 %collective-permute-start.9 = (bf16[4,2,4,72,128]{4,3,2,1,0:T(8,128)(2,1)S(1)}, bf16[4,2,4,72,128]{4,3,2,1,0:T(8,128)(2,1)S(1)}, u32[]{:S(2)}, u32[]{:S(2)}) collective-permute-start(bf16[4,2,4,72,128]{4,3,2,1,0:T(8,128)(2,1)S(1)} %bitcast.44), channel_id=1, source_target_pairs={{0,1},{1,0},{2,3},{3,2},{4,5},{5,4},{6,7},{7,6},{8,9},{9,8},{10,11... | collective-permute-start | bytes 1769480 | tf_op jit(solution)/shard_map/ppermute | solution.py:33
  78.8 2.3 %collective-permute-done.10.refs_2_ = bf16[4,2,4,72,128]{4,3,2,1,0:T(8,128)(2,1)S(1)} collective-permute-done((bf16[4,2,4,72,128]{4,3,2,1,0:T(8,128)(2,1)S(1)}, bf16[4,2,4,72,128]{4,3,2,1,0:T(8,128)(2,1)S(1)}, u32[]{:S(2)}, u32[]{:S(2)}) %collective-permute-start.10) | collective-permute-done | bytes 589856 | tf_op jit(solution)/shard_map/ppermute | solution.py:37
  81.2 1.5 collective-permute-start.16
  82.6 2.7 %collective-permute-start.18 = (bf16[16,128,128]{2,1,0:T(8,128)(2,1)S(1)}, bf16[16,128,128]{2,1,0:T(8,128)(2,1)S(1)}, u32[]{:S(2)}, u32[]{:S(2)}) collective-permute-start(bf16[16,128,128]{2,1,0:T(8,128)(2,1)S(1)} %slice.177), channel_id=1, source_target_pairs={{0,6},{1,7},{2,0},{3,1},{4,2},{5,3},{6,4},{7,5},{8,14},{9,15},{10,... | collective-permute-start | bytes 1572872 | tf_op jit(solution)/shard_map/ppermute | solution.py:41
  85.4 6.7 %collective-permute-done.17.refs_14_ = bf16[16,128,128]{2,1,0:T(8,128)(2,1)S(1)} collective-permute-done((bf16[16,128,128]{2,1,0:T(8,128)(2,1)S(1)}, bf16[16,128,128]{2,1,0:T(8,128)(2,1)S(1)}, u32[]{:S(2)}, u32[]{:S(2)}) %collective-permute-start.17) | collective-permute-done | bytes 524320 | tf_op jit(solution)/shard_map/ppermute | solution.py:41
  92.2 1.5 collective-permute-done.16.refs_6_
  93.6 7.2 %collective-permute-start.23 = (bf16[2,144,2048]{2,1,0:T(8,128)(2,1)S(1)}, bf16[2,144,2048]{2,1,0:T(8,128)(2,1)S(1)}, u32[]{:S(2)}, u32[]{:S(2)}) collective-permute-start(bf16[2,144,2048]{2,1,0:T(8,128)(2,1)S(1)} %constant_dynamic-update-slice_fusion.refs_10_), channel_id=1, source_target_pairs={{0,1},{1,0},{2,3},{3,2},{4,5},{5,4},{6,7},{7,6},{8,9},{9,8},{10,11... | collective-permute-start | bytes 3538952 | tf_op jit(solution)/shard_map/ppermute | solution.py:33
  101.5 2.7 %collective-permute-done.20.refs_3_ = bf16[4,2,4,72,128]{4,3,2,1,0:T(8,128)(2,1)S(1)} collective-permute-done((bf16[4,2,4,72,128]{4,3,2,1,0:T(8,128)(2,1)S(1)}, bf16[4,2,4,72,128]{4,3,2,1,0:T(8,128)(2,1)S(1)}, u32[]{:S(2)}, u32[]{:S(2)}) %collective-permute-start.20) | collective-permute-done | bytes 589856 | tf_op jit(solution)/shard_map/ppermute | solution.py:33
  104.2 0.8 collective-permute-done.21.refs_5_
  105.0 0.8 collective-permute-done.22.refs_7_
  105.9 26.7 %window_pass.1 = (bf16[2,4,2,4,144,128]{5,4,3,2,1,0:T(8,128)(2,1)S(1)}, bf16[4,2,4,144,128]{4,3,2,1,0:T(8,128)(2,1)S(1)}, bf16[4,2,4,144,128]{4,3,2,1,0:T(8,128)...) custom-call(s32[4]{0:T(128)S(1)} %copy-done.1, ...), custom_call_target="tpu_custom_call" | custom-call | flops 32000000000 | bytes 30000000 | tf_op jit(solution)/shard_map/window_pass/pallas_call | solution.py:358
  133.0 1.3 collective-permute-start.32
  134.5 2.8 %collective-permute-done.24 = bf16[2,4,2,4,144,128]{5,4,3,2,1,0:T(8,128)(2,1)S(1)} collective-permute-done((bf16[2,4,2,4,144,128]{5,4,3,2,1,0:T(8,128)(2,1)S(1)}, bf16[2,4,2,4,144,128]{5,4,3,2,1,0:T(8,128)(2,1)S(1)}, u32[]{:S(2)}, u32[]{:S(2)}) %collective-permute-start.24) | collective-permute-done | bytes 2359328 | tf_op jit(solution)/shard_map/ppermute | solution.py:33
  137.3 0.6 fusion
  137.9 1.8 collective-permute-start.25
  140.0 17.6 %collective-permute-done.32 = bf16[32,128,128]{2,1,0:T(8,128)(2,1)S(1)} collective-permute-done((bf16[32,128,128]{2,1,0:T(8,128)(2,1)S(1)}, bf16[32,128,128]{2,1,0:T(8,128)(2,1)S(1)}, u32[]{:S(2)}, u32[]{:S(2)}) %collective-permute-start.32) | collective-permute-done | bytes 1048608 | tf_op jit(solution)/shard_map/ppermute | solution.py:41
  157.7 2.1 %collective-permute-done.33 = bf16[32,128,128]{2,1,0:T(8,128)(2,1)S(1)} collective-permute-done((bf16[32,128,128]{2,1,0:T(8,128)(2,1)S(1)}, bf16[32,128,128]{2,1,0:T(8,128)(2,1)S(1)}, u32[]{:S(2)}, u32[]{:S(2)}) %collective-permute-start.33) | collective-permute-done | bytes 1048608 | tf_op jit(solution)/shard_map/ppermute | solution.py:41
  160.2 0.5 collective-permute-start.34
  160.7 1.0 collective-permute-start.35
  161.7 1.2 collective-permute-start.27
  162.9 4.5 %collective-permute-start.28 = (bf16[4,2,4,72,128]{4,3,2,1,0:T(8,128)(2,1)S(1)}, bf16[4,2,4,72,128]{4,3,2,1,0:T(8,128)(2,1)S(1)}, u32[]{:S(2)}, u32[]{:S(2)}) collective-permute-start(bf16[4,2,4,72,128]{4,3,2,1,0:T(8,128)(2,1)S(1)} %add_convert_fusion), channel_id=1, source_target_pairs={{0,32},{1,33},{2,34},{3,35},{4,36},{5,37},{6,38},{7,39},{8,40},{9,... | collective-permute-start | bytes 1769480 | tf_op jit(solution)/shard_map/ppermute | solution.py:49
  167.5 4.9 %collective-permute-done.34 = bf16[16,128,128]{2,1,0:T(8,128)(2,1)S(1)} collective-permute-done((bf16[16,128,128]{2,1,0:T(8,128)(2,1)S(1)}, bf16[16,128,128]{2,1,0:T(8,128)(2,1)S(1)}, u32[]{:S(2)}, u32[]{:S(2)}) %collective-permute-start.34) | collective-permute-done | bytes 524320 | tf_op jit(solution)/shard_map/ppermute | solution.py:41
  172.3 1.7 collective-permute-done.35
  174.8 1.3 collective-permute-start.36
  176.3 2.3 %collective-permute-done.28 = bf16[4,2,4,72,128]{4,3,2,1,0:T(8,128)(2,1)S(1)} collective-permute-done((bf16[4,2,4,72,128]{4,3,2,1,0:T(8,128)(2,1)S(1)}, bf16[4,2,4,72,128]{4,3,2,1,0:T(8,128)(2,1)S(1)}, u32[]{:S(2)}, u32[]{:S(2)}) %collective-permute-start.28) | collective-permute-done | bytes 589856 | tf_op jit(solution)/shard_map/ppermute | solution.py:49
  179.1 2.4 %collective-permute-start.29 = (bf16[2,4,144,128]{3,2,1,0:T(8,128)(2,1)S(1)}, bf16[2,4,144,128]{3,2,1,0:T(8,128)(2,1)S(1)}, u32[]{:S(2)}, u32[]{:S(2)}) collective-permute-start(bf16[2,4,144,128]{3,2,1,0:T(8,128)(2,1)S(1)} %get-tuple-element.82), channel_id=1, source_target_pairs={{0,6},{1,7},{2,0},{3,1},{4,2},{5,3},{6,4},{7,5},{8,14},{9,15},{10,... | collective-permute-start | bytes 884744 | tf_op jit(solution)/shard_map/ppermute | solution.py:41
  182.0 3.9 %collective-permute-done.31 = bf16[2,4,144,128]{3,2,1,0:T(8,128)(2,1)S(1)} collective-permute-done((bf16[2,4,144,128]{3,2,1,0:T(8,128)(2,1)S(1)}, bf16[2,4,144,128]{3,2,1,0:T(8,128)(2,1)S(1)}, u32[]{:S(2)}, u32[]{:S(2)}) %collective-permute-start.31) | collective-permute-done | bytes 294944 | tf_op jit(solution)/shard_map/ppermute | solution.py:41
  185.9 1.3 collective-permute-done.29
  187.1 5.2 %collective-permute-done.30 = bf16[2,4,144,128]{3,2,1,0:T(8,128)(2,1)S(1)} collective-permute-done((bf16[2,4,144,128]{3,2,1,0:T(8,128)(2,1)S(1)}, bf16[2,4,144,128]{3,2,1,0:T(8,128)(2,1)S(1)}, u32[]{:S(2)}, u32[]{:S(2)}) %collective-permute-start.30) | collective-permute-done | bytes 294944 | tf_op jit(solution)/shard_map/ppermute | solution.py:41
  192.4 4.0 %collective-permute-start.37 = (bf16[2,6,128,128]{3,2,1,0:T(8,128)(2,1)S(1)}, bf16[2,6,128,128]{3,2,1,0:T(8,128)(2,1)S(1)}, u32[]{:S(2)}, u32[]{:S(2)}) collective-permute-start(bf16[2,6,128,128]{3,2,1,0:T(8,128)(2,1)S(1)} %pad_maximum_fusion.6), channel_id=1, source_target_pairs={{0,1},{1,0},{2,3},{3,2},{4,5},{5,4},{6,7},{7,6},{8,9},{9,8},{10,11... | collective-permute-start | bytes 1179656 | tf_op jit(solution)/shard_map/ppermute | solution.py:33
  196.9 1.2 broadcast_in_dim_reshape.3
  198.1 1.9 token_join.1
  200.0 0.8 copy-done.8
  200.7 3.5 %weight_join.1 = f32[128,3072]{1,0:T(8,128)} custom-call(s32[4]{0:T(128)} %pad_add_fusion.s_ref, f32[32,128,128]{2,1,0:T(8,128)} %copy-done.2, bf16[2,6,128,128]{3,2,1,0:T(8,128)(2,1)} %copy-done.8, bf16[2,6,128,128]{3,2,1,0:T(8,128)(2,1)} %copy-done.4), custom_call_target="tpu_custom_call" | custom-call | bytes 3000000 | tf_op jit(solution)/shard_map/weight_join/pallas_call | solution.py:126
  (83 shorter events, 7.0 us)
Async XLA Ops:
  0.6 6.5 %copy-start = (bf16[12,192,2,128]{3,2,1,0:T(2,128)(2,1)S(1)}, bf16[12,192,2,128]{3,2,1,0:T(2,128)(2,1)}, u32[]{:S(2)}) copy-start(bf16[12,192,2,128]{3,2,1,0:T(2,128)(2,1)} %high_ref.1) | copy-start | bytes 3538948
  4.4 9.7 %copy-start.5 = (bf16[4,6,128,128]{3,2,1,0:T(8,128)(2,1)S(1)}, bf16[4,6,128,128]{3,2,1,0:T(8,128)(2,1)}, u32[]{:S(2)}) copy-start(bf16[4,6,128,128]{3,2,1,0:T(8,128)(2,1)} %get-tuple-element.41) | copy-start | bytes 2359300
  5.6 12.0 %collective-permute-start.2 = (bf16[12,3,2,2048]{3,2,1,0:T(2,128)(2,1)S(1)}, bf16[12,3,2,2048]{3,2,1,0:T(2,128)(2,1)S(1)}, u32[]{:S(2)}, u32[]{:S(2)}) collective-permute-start(bf16[12,3,2,2048]{3,2,1,0:T(2,128)(2,1)S(1)} %slice.132), channel_id=1, source_target_pairs={{0,15},{1,0},{2,1},{3,2},{4,3},{5,4},{6,5},{7,6},{8,7},{9,8},{10,9... | collective-permute-start | bytes 884744 | tf_op jit(solution)/shard_map/ppermute | solution.py:62
  8.3 23.4 %collective-permute-start.3 = (bf16[6,192,2,128]{3,2,1,0:T(2,128)(2,1)}, bf16[6,192,2,128]{3,2,1,0:T(2,128)(2,1)S(1)}, u32[]{:S(2)}, u32[]{:S(2)}) collective-permute-start(bf16[6,192,2,128]{3,2,1,0:T(2,128)(2,1)} %slice.135), channel_id=1, source_target_pairs={{0,96},{1,97},{2,98},{3,99},{4,100},{5,101},{6,102},{7,103},{8,104... | collective-permute-start | bytes 1769480 | tf_op jit(solution)/shard_map/ppermute | solution.py:49
  14.1 3.5 %slice-start = ((bf16[12,12,2,2048]{3,2,1,0:T(2,128)(2,1)}), bf16[12,9,2,2048]{3,2,1,0:T(2,128)(2,1)S(1)}, s32[]{:S(2)}) async-start(bf16[12,12,2,2048]{3,2,1,0:T(2,128)(2,1)} %param.5), calls=%async_computation | async-start | bytes 1769472 | tf_op jit(solution)/shard_map/slice | solution.py:403
  14.1 8.6 %collective-permute-start = (bf16[2,6,128,128]{3,2,1,0:T(8,128)(2,1)S(1)}, bf16[2,6,128,128]{3,2,1,0:T(8,128)(2,1)S(1)}, u32[]{:S(2)}, u32[]{:S(2)}) collective-permute-start(bf16[2,6,128,128]{3,2,1,0:T(8,128)(2,1)S(1)} %stack.39), channel_id=1, source_target_pairs={{0,8},{1,9},{2,10},{3,11},{4,12},{5,13},{6,14},{7,15},{8,0},{9,1},... | collective-permute-start | bytes 1179656 | tf_op jit(solution)/shard_map/ppermute | solution.py:37
  24.2 14.4 %collective-permute-start.1 = (bf16[2,6,128,128]{3,2,1,0:T(8,128)(2,1)}, bf16[2,6,128,128]{3,2,1,0:T(8,128)(2,1)}, u32[]{:S(2)}, u32[]{:S(2)}) collective-permute-start(bf16[2,6,128,128]{3,2,1,0:T(8,128)(2,1)} %pad_maximum_fusion.5), channel_id=1, source_target_pairs={{0,1},{1,0},{2,3},{3,2},{4,5},{5,4},{6,7},{7,6},{8,9},{9,8},{10,11... | collective-permute-start | bytes 1179656 | tf_op jit(solution)/shard_map/ppermute | solution.py:33
  31.2 0.6 copy-start.1
  31.7 9.7 %copy-start.6 = (bf16[6,128,128]{2,1,0:T(8,128)(2,1)S(1)}, bf16[6,128,128]{2,1,0:T(8,128)(2,1)}, u32[]{:S(2)}) copy-start(bf16[6,128,128]{2,1,0:T(8,128)(2,1)} %get-tuple-element.89) | copy-start | bytes 589828
  31.7 9.7 %copy-start.7 = (bf16[6,128,128]{2,1,0:T(8,128)(2,1)S(1)}, bf16[6,128,128]{2,1,0:T(8,128)(2,1)}, u32[]{:S(2)}) copy-start(bf16[6,128,128]{2,1,0:T(8,128)(2,1)} %get-tuple-element.91) | copy-start | bytes 589828
  31.7 9.7 %copy-start.9 = (bf16[8,128,128]{2,1,0:T(8,128)(2,1)S(1)}, bf16[8,128,128]{2,1,0:T(8,128)(2,1)}, u32[]{:S(2)}) copy-start(bf16[8,128,128]{2,1,0:T(8,128)(2,1)} %get-tuple-element.42) | copy-start | bytes 786436
  32.7 10.1 %collective-permute-start.5 = (bf16[2,2,4,6,6,2,128]{6,5,4,3,2,1,0:T(2,128)(2,1)S(1)}, bf16[2,2,4,6,6,2,128]{6,5,4,3,2,1,0:T(2,128)(2,1)S(1)}, u32[]{:S(2)}, u32[]{:S(2)}) collective-permute-start(bf16[2,2,4,6,6,2,128]{6,5,4,3,2,1,0:T(2,128)(2,1)S(1)} %get-tuple-element.50), channel_id=1, source_target_pairs={{0,2},{1,3},{2,4},{3,5},{4,6},{5,7},{6,0},{7,1},{8,10},{9,11},{10,... | collective-permute-start | bytes 884744 | tf_op jit(solution)/shard_map/ppermute | solution.py:41
  32.8 16.0 %collective-permute-start.6 = (bf16[2,2,4,6,6,2,128]{6,5,4,3,2,1,0:T(2,128)(2,1)S(1)}, bf16[2,2,4,6,6,2,128]{6,5,4,3,2,1,0:T(2,128)(2,1)S(1)}, u32[]{:S(2)}, u32[]{:S(2)}) collective-permute-start(bf16[2,2,4,6,6,2,128]{6,5,4,3,2,1,0:T(2,128)(2,1)S(1)} %get-tuple-element.51), channel_id=1, source_target_pairs={{0,4},{1,5},{2,6},{3,7},{4,0},{5,1},{6,2},{7,3},{8,12},{9,13},{10,... | collective-permute-start | bytes 884744 | tf_op jit(solution)/shard_map/ppermute | solution.py:41
  35.2 14.0 %collective-permute-start.7 = (bf16[2,2,4,6,6,2,128]{6,5,4,3,2,1,0:T(2,128)(2,1)S(1)}, bf16[2,2,4,6,6,2,128]{6,5,4,3,2,1,0:T(2,128)(2,1)S(1)}, u32[]{:S(2)}, u32[]{:S(2)}) collective-permute-start(bf16[2,2,4,6,6,2,128]{6,5,4,3,2,1,0:T(2,128)(2,1)S(1)} %get-tuple-element.52), channel_id=1, source_target_pairs={{0,6},{1,7},{2,0},{3,1},{4,2},{5,3},{6,4},{7,5},{8,14},{9,15},{10,... | collective-permute-start | bytes 884744 | tf_op jit(solution)/shard_map/ppermute | solution.py:41
  36.3 15.9 %collective-permute-start.4 = (bf16[2,72,2048]{2,1,0:T(8,128)(2,1)S(1)}, bf16[2,72,2048]{2,1,0:T(8,128)(2,1)S(1)}, u32[]{:S(2)}, u32[]{:S(2)}) collective-permute-start(bf16[2,72,2048]{2,1,0:T(8,128)(2,1)S(1)} %squeeze.25), channel_id=1, source_target_pairs={{0,96},{1,97},{2,98},{3,99},{4,100},{5,101},{6,102},{7,103},{8,104... | collective-permute-start | bytes 1769480 | tf_op jit(solution)/shard_map/ppermute | solution.py:49
  38.6 14.6 %collective-permute-start.8 = (bf16[2,72,2048]{2,1,0:T(8,128)(2,1)S(1)}, bf16[2,72,2048]{2,1,0:T(8,128)(2,1)S(1)}, u32[]{:S(2)}, u32[]{:S(2)}) collective-permute-start(bf16[2,72,2048]{2,1,0:T(8,128)(2,1)S(1)} %squeeze.26), channel_id=1, source_target_pairs={{0,8},{1,9},{2,10},{3,11},{4,12},{5,13},{6,14},{7,15},{8,0},{9,1},... | collective-permute-start | bytes 1769480 | tf_op jit(solution)/shard_map/ppermute | solution.py:37
  53.1 22.3 %collective-permute-start.12 = (bf16[32,128,128]{2,1,0:T(8,128)(2,1)S(1)}, bf16[32,128,128]{2,1,0:T(8,128)(2,1)S(1)}, u32[]{:S(2)}, u32[]{:S(2)}) collective-permute-start(bf16[32,128,128]{2,1,0:T(8,128)(2,1)S(1)} %pad_maximum_fusion.2.refs_12_), channel_id=1, source_target_pairs={{0,6},{1,7},{2,0},{3,1},{4,2},{5,3},{6,4},{7,5},{8,14},{9,15},{10,... | collective-permute-start | bytes 3145736 | tf_op jit(solution)/shard_map/ppermute | solution.py:41
  54.7 12.9 %collective-permute-start.14 = (bf16[2,72,2048]{2,1,0:T(8,128)(2,1)S(1)}, bf16[2,72,2048]{2,1,0:T(8,128)(2,1)S(1)}, u32[]{:S(2)}, u32[]{:S(2)}) collective-permute-start(bf16[2,72,2048]{2,1,0:T(8,128)(2,1)S(1)} %collective-permute-done.4), channel_id=1, source_target_pairs={{0,16},{1,17},{2,18},{3,19},{4,20},{5,21},{6,22},{7,23},{8,24},{9,... | collective-permute-start | bytes 1769480 | tf_op jit(solution)/shard_map/ppermute | solution.py:58
  54.7 24.1 %collective-permute-start.11 = (bf16[32,128,128]{2,1,0:T(8,128)(2,1)S(1)}, bf16[32,128,128]{2,1,0:T(8,128)(2,1)S(1)}, u32[]{:S(2)}, u32[]{:S(2)}) collective-permute-start(bf16[32,128,128]{2,1,0:T(8,128)(2,1)S(1)} %pad_maximum_fusion.2.refs_12_), channel_id=1, source_target_pairs={{0,2},{1,3},{2,4},{3,5},{4,6},{5,7},{6,0},{7,1},{8,10},{9,11},{10,... | collective-permute-start | bytes 3145736 | tf_op jit(solution)/shard_map/ppermute | solution.py:41
  54.7 24.1 %collective-permute-start.13 = (bf16[2,72,2048]{2,1,0:T(8,128)(2,1)S(1)}, bf16[2,72,2048]{2,1,0:T(8,128)(2,1)S(1)}, u32[]{:S(2)}, u32[]{:S(2)}) collective-permute-start(bf16[2,72,2048]{2,1,0:T(8,128)(2,1)S(1)} %collective-permute-done.4), channel_id=1, source_target_pairs={{0,24},{1,25},{2,26},{3,27},{4,28},{5,29},{6,30},{7,31},{8,16},{9,... | collective-permute-start | bytes 1769480 | tf_op jit(solution)/shard_map/ppermute | solution.py:58
  57.7 23.4 %collective-permute-start.10 = (bf16[4,2,4,72,128]{4,3,2,1,0:T(8,128)(2,1)S(1)}, bf16[4,2,4,72,128]{4,3,2,1,0:T(8,128)(2,1)S(1)}, u32[]{:S(2)}, u32[]{:S(2)}) collective-permute-start(bf16[4,2,4,72,128]{4,3,2,1,0:T(8,128)(2,1)S(1)} %bitcast.43), channel_id=1, source_target_pairs={{0,8},{1,9},{2,10},{3,11},{4,12},{5,13},{6,14},{7,15},{8,0},{9,1},... | collective-permute-start | bytes 1769480 | tf_op jit(solution)/shard_map/ppermute | solution.py:37
  67.6 26.0 %collective-permute-start.19 = (bf16[2,144,2048]{2,1,0:T(8,128)(2,1)S(1)}, bf16[2,144,2048]{2,1,0:T(8,128)(2,1)S(1)}, u32[]{:S(2)}, u32[]{:S(2)}) collective-permute-start(bf16[2,144,2048]{2,1,0:T(8,128)(2,1)S(1)} %constant_dynamic-update-slice_fusion.2.refs_8_), channel_id=1, source_target_pairs={{0,1},{1,0},{2,3},{3,2},{4,5},{5,4},{6,7},{7,6},{8,9},{9,8},{10,11... | collective-permute-start | bytes 3538952 | tf_op jit(solution)/shard_map/ppermute | solution.py:33
  75.5 7.2 %collective-permute-start.9 = (bf16[4,2,4,72,128]{4,3,2,1,0:T(8,128)(2,1)S(1)}, bf16[4,2,4,72,128]{4,3,2,1,0:T(8,128)(2,1)S(1)}, u32[]{:S(2)}, u32[]{:S(2)}) collective-permute-start(bf16[4,2,4,72,128]{4,3,2,1,0:T(8,128)(2,1)S(1)} %bitcast.44), channel_id=1, source_target_pairs={{0,1},{1,0},{2,3},{3,2},{4,5},{5,4},{6,7},{7,6},{8,9},{9,8},{10,11... | collective-permute-start | bytes 1769480 | tf_op jit(solution)/shard_map/ppermute | solution.py:33
  81.2 12.5 %collective-permute-start.16 = (bf16[4,2,4,72,128]{4,3,2,1,0:T(8,128)(2,1)S(1)}, bf16[4,2,4,72,128]{4,3,2,1,0:T(8,128)(2,1)S(1)}, u32[]{:S(2)}, u32[]{:S(2)}) collective-permute-start(bf16[4,2,4,72,128]{4,3,2,1,0:T(8,128)(2,1)S(1)} %bitcast.53), channel_id=1, source_target_pairs={{0,24},{1,25},{2,26},{3,27},{4,28},{5,29},{6,30},{7,31},{8,16},{9,... | collective-permute-start | bytes 1769480 | tf_op jit(solution)/shard_map/ppermute | solution.py:58
  82.6 11.0 %collective-permute-start.15 = (bf16[4,2,4,72,128]{4,3,2,1,0:T(8,128)(2,1)S(1)}, bf16[4,2,4,72,128]{4,3,2,1,0:T(8,128)(2,1)S(1)}, u32[]{:S(2)}, u32[]{:S(2)}) collective-permute-start(bf16[4,2,4,72,128]{4,3,2,1,0:T(8,128)(2,1)S(1)} %bitcast.54), channel_id=1, source_target_pairs={{0,16},{1,17},{2,18},{3,19},{4,20},{5,21},{6,22},{7,23},{8,24},{9,... | collective-permute-start | bytes 1769480 | tf_op jit(solution)/shard_map/ppermute | solution.py:58
  82.6 9.5 %collective-permute-start.17 = (bf16[16,128,128]{2,1,0:T(8,128)(2,1)S(1)}, bf16[16,128,128]{2,1,0:T(8,128)(2,1)S(1)}, u32[]{:S(2)}, u32[]{:S(2)}) collective-permute-start(bf16[16,128,128]{2,1,0:T(8,128)(2,1)S(1)} %slice.176), channel_id=1, source_target_pairs={{0,2},{1,3},{2,4},{3,5},{4,6},{5,7},{6,0},{7,1},{8,10},{9,11},{10,... | collective-permute-start | bytes 1572872 | tf_op jit(solution)/shard_map/ppermute | solution.py:41
  82.6 9.5 %collective-permute-start.18 = (bf16[16,128,128]{2,1,0:T(8,128)(2,1)S(1)}, bf16[16,128,128]{2,1,0:T(8,128)(2,1)S(1)}, u32[]{:S(2)}, u32[]{:S(2)}) collective-permute-start(bf16[16,128,128]{2,1,0:T(8,128)(2,1)S(1)} %slice.177), channel_id=1, source_target_pairs={{0,6},{1,7},{2,0},{3,1},{4,2},{5,3},{6,4},{7,5},{8,14},{9,15},{10,... | collective-permute-start | bytes 1572872 | tf_op jit(solution)/shard_map/ppermute | solution.py:41
  93.6 12.3 %collective-permute-start.23 = (bf16[2,144,2048]{2,1,0:T(8,128)(2,1)S(1)}, bf16[2,144,2048]{2,1,0:T(8,128)(2,1)S(1)}, u32[]{:S(2)}, u32[]{:S(2)}) collective-permute-start(bf16[2,144,2048]{2,1,0:T(8,128)(2,1)S(1)} %constant_dynamic-update-slice_fusion.refs_10_), channel_id=1, source_target_pairs={{0,1},{1,0},{2,3},{3,2},{4,5},{5,4},{6,7},{7,6},{8,9},{9,8},{10,11... | collective-permute-start | bytes 3538952 | tf_op jit(solution)/shard_map/ppermute | solution.py:33
  100.9 3.3 %collective-permute-start.20 = (bf16[4,2,4,72,128]{4,3,2,1,0:T(8,128)(2,1)S(1)}, bf16[4,2,4,72,128]{4,3,2,1,0:T(8,128)(2,1)S(1)}, u32[]{:S(2)}, u32[]{:S(2)}) collective-permute-start(bf16[4,2,4,72,128]{4,3,2,1,0:T(8,128)(2,1)S(1)} %collective-permute-done.10.refs_2_), channel_id=1, source_target_pairs={{0,1},{1,0},{2,3},{3,2},{4,5},{5,4},{6,7},{7,6},{8,9},{9,8},{10,11... | collective-permute-start | bytes 1769480 | tf_op jit(solution)/shard_map/ppermute | solution.py:33
  101.0 4.1 %collective-permute-start.21 = (bf16[4,2,4,72,128]{4,3,2,1,0:T(8,128)(2,1)S(1)}, bf16[4,2,4,72,128]{4,3,2,1,0:T(8,128)(2,1)S(1)}, u32[]{:S(2)}, u32[]{:S(2)}) collective-permute-start(bf16[4,2,4,72,128]{4,3,2,1,0:T(8,128)(2,1)S(1)} %collective-permute-done.15.refs_4_), channel_id=1, source_target_pairs={{0,1},{1,0},{2,3},{3,2},{4,5},{5,4},{6,7},{7,6},{8,9},{9,8},{10,11... | collective-permute-start | bytes 1769480 | tf_op jit(solution)/shard_map/ppermute | solution.py:33
  101.4 4.5 %collective-permute-start.22 = (bf16[4,2,4,72,128]{4,3,2,1,0:T(8,128)(2,1)S(1)}, bf16[4,2,4,72,128]{4,3,2,1,0:T(8,128)(2,1)S(1)}, u32[]{:S(2)}, u32[]{:S(2)}) collective-permute-start(bf16[4,2,4,72,128]{4,3,2,1,0:T(8,128)(2,1)S(1)} %collective-permute-done.16.refs_6_), channel_id=1, source_target_pairs={{0,1},{1,0},{2,3},{3,2},{4,5},{5,4},{6,7},{7,6},{8,9},{9,8},{10,11... | collective-permute-start | bytes 1769480 | tf_op jit(solution)/shard_map/ppermute | solution.py:33
  132.6 4.6 %collective-permute-start.24 = (bf16[2,4,2,4,144,128]{5,4,3,2,1,0:T(8,128)(2,1)S(1)}, bf16[2,4,2,4,144,128]{5,4,3,2,1,0:T(8,128)(2,1)S(1)}, u32[]{:S(2)}, u32[]{:S(2)}) collective-permute-start(bf16[2,4,2,4,144,128]{5,4,3,2,1,0:T(8,128)(2,1)S(1)} %get-tuple-element.66), channel_id=1, source_target_pairs={{0,1},{1,0},{2,3},{3,2},{4,5},{5,4},{6,7},{7,6},{8,9},{9,8},{10,11... | collective-permute-start | bytes 7077896 | tf_op jit(solution)/shard_map/ppermute | solution.py:33
  133.0 24.5 %collective-permute-start.32 = (bf16[32,128,128]{2,1,0:T(8,128)(2,1)S(1)}, bf16[32,128,128]{2,1,0:T(8,128)(2,1)S(1)}, u32[]{:S(2)}, u32[]{:S(2)}) collective-permute-start(bf16[32,128,128]{2,1,0:T(8,128)(2,1)S(1)} %get-tuple-element.72), channel_id=1, source_target_pairs={{0,6},{1,7},{2,0},{3,1},{4,2},{5,3},{6,4},{7,5},{8,14},{9,15},{10,... | collective-permute-start | bytes 3145736 | tf_op jit(solution)/shard_map/ppermute | solution.py:41
  134.3 25.5 %collective-permute-start.33 = (bf16[32,128,128]{2,1,0:T(8,128)(2,1)S(1)}, bf16[32,128,128]{2,1,0:T(8,128)(2,1)S(1)}, u32[]{:S(2)}, u32[]{:S(2)}) collective-permute-start(bf16[32,128,128]{2,1,0:T(8,128)(2,1)S(1)} %get-tuple-element.74), channel_id=1, source_target_pairs={{0,2},{1,3},{2,4},{3,5},{4,6},{5,7},{6,0},{7,1},{8,10},{9,11},{10,... | collective-permute-start | bytes 3145736 | tf_op jit(solution)/shard_map/ppermute | solution.py:41
  137.9 22.1 %collective-permute-start.25 = (bf16[4,2,4,72,128]{4,3,2,1,0:T(8,128)(2,1)S(1)}, bf16[4,2,4,72,128]{4,3,2,1,0:T(8,128)(2,1)S(1)}, u32[]{:S(2)}, u32[]{:S(2)}) collective-permute-start(bf16[4,2,4,72,128]{4,3,2,1,0:T(8,128)(2,1)S(1)} %slice.243), channel_id=1, source_target_pairs={{0,16},{1,17},{2,18},{3,19},{4,20},{5,21},{6,22},{7,23},{8,24},{9,... | collective-permute-start | bytes 1769480 | tf_op jit(solution)/shard_map/ppermute | solution.py:58
  139.9 20.1 %collective-permute-start.26 = (bf16[4,2,4,72,128]{4,3,2,1,0:T(8,128)(2,1)S(1)}, bf16[4,2,4,72,128]{4,3,2,1,0:T(8,128)(2,1)S(1)}, u32[]{:S(2)}, u32[]{:S(2)}) collective-permute-start(bf16[4,2,4,72,128]{4,3,2,1,0:T(8,128)(2,1)S(1)} %get-tuple-element.85), channel_id=1, source_target_pairs={{0,24},{1,25},{2,26},{3,27},{4,28},{5,29},{6,30},{7,31},{8,16},{9,... | collective-permute-start | bytes 1769480 | tf_op jit(solution)/shard_map/ppermute | solution.py:58
  157.6 9.8 %copy-start.3 = (bf16[32,128,128]{2,1,0:T(8,128)(2,1)}, bf16[32,128,128]{2,1,0:T(8,128)(2,1)S(1)}, u32[]{:S(2)}) copy-start(bf16[32,128,128]{2,1,0:T(8,128)(2,1)S(1)} %collective-permute-done.32) | copy-start | bytes 3145732
  160.2 12.2 %collective-permute-start.34 = (bf16[16,128,128]{2,1,0:T(8,128)(2,1)S(1)}, bf16[16,128,128]{2,1,0:T(8,128)(2,1)S(1)}, u32[]{:S(2)}, u32[]{:S(2)}) collective-permute-start(bf16[16,128,128]{2,1,0:T(8,128)(2,1)S(1)} %add_convert_fusion.2), channel_id=1, source_target_pairs={{0,6},{1,7},{2,0},{3,1},{4,2},{5,3},{6,4},{7,5},{8,14},{9,15},{10,... | collective-permute-start | bytes 1572872 | tf_op jit(solution)/shard_map/ppermute | solution.py:41
  160.7 13.4 %collective-permute-start.35 = (bf16[16,128,128]{2,1,0:T(8,128)(2,1)S(1)}, bf16[16,128,128]{2,1,0:T(8,128)(2,1)S(1)}, u32[]{:S(2)}, u32[]{:S(2)}) collective-permute-start(bf16[16,128,128]{2,1,0:T(8,128)(2,1)S(1)} %add_convert_fusion.1), channel_id=1, source_target_pairs={{0,2},{1,3},{2,4},{3,5},{4,6},{5,7},{6,0},{7,1},{8,10},{9,11},{10,... | collective-permute-start | bytes 1572872 | tf_op jit(solution)/shard_map/ppermute | solution.py:41
  161.7 14.5 %collective-permute-start.27 = (bf16[4,2,4,72,128]{4,3,2,1,0:T(8,128)(2,1)S(1)}, bf16[4,2,4,72,128]{4,3,2,1,0:T(8,128)(2,1)S(1)}, u32[]{:S(2)}, u32[]{:S(2)}) collective-permute-start(bf16[4,2,4,72,128]{4,3,2,1,0:T(8,128)(2,1)S(1)} %get-tuple-element.68), channel_id=1, source_target_pairs={{0,8},{1,9},{2,10},{3,11},{4,12},{5,13},{6,14},{7,15},{8,0},{9,1},... | collective-permute-start | bytes 1769480 | tf_op jit(solution)/shard_map/ppermute | solution.py:37
  162.9 15.8 %collective-permute-start.28 = (bf16[4,2,4,72,128]{4,3,2,1,0:T(8,128)(2,1)S(1)}, bf16[4,2,4,72,128]{4,3,2,1,0:T(8,128)(2,1)S(1)}, u32[]{:S(2)}, u32[]{:S(2)}) collective-permute-start(bf16[4,2,4,72,128]{4,3,2,1,0:T(8,128)(2,1)S(1)} %add_convert_fusion), channel_id=1, source_target_pairs={{0,32},{1,33},{2,34},{3,35},{4,36},{5,37},{6,38},{7,39},{8,40},{9,... | collective-permute-start | bytes 1769480 | tf_op jit(solution)/shard_map/ppermute | solution.py:49
  167.4 6.7 %slice-start.1 = ((bf16[32,128,128]{2,1,0:T(8,128)(2,1)}), bf16[16,128,128]{2,1,0:T(8,128)(2,1)S(1)}, s32[]{:S(2)}) async-start(bf16[32,128,128]{2,1,0:T(8,128)(2,1)} %copy-done.3), calls=%async_computation.1 | async-start | bytes 1048576 | tf_op jit(solution)/shard_map/slice | solution.py:452
  174.6 21.9 %copy-start.2 = (f32[32,128,128]{2,1,0:T(8,128)}, f32[32,128,128]{2,1,0:T(8,128)S(1)}, u32[]{:S(2)}) copy-start(f32[32,128,128]{2,1,0:T(8,128)S(1)} %convert_add_fusion.2.a_ref) | copy-start | bytes 6291460
  174.8 17.5 %collective-permute-start.36 = (bf16[2,6,128,128]{3,2,1,0:T(8,128)(2,1)S(1)}, bf16[2,6,128,128]{3,2,1,0:T(8,128)(2,1)S(1)}, u32[]{:S(2)}, u32[]{:S(2)}) collective-permute-start(bf16[2,6,128,128]{3,2,1,0:T(8,128)(2,1)S(1)} %bitcast.55), channel_id=1, source_target_pairs={{0,8},{1,9},{2,10},{3,11},{4,12},{5,13},{6,14},{7,15},{8,0},{9,1},... | collective-permute-start | bytes 1179656 | tf_op jit(solution)/shard_map/ppermute | solution.py:37
  178.7 7.1 %collective-permute-start.31 = (bf16[2,4,144,128]{3,2,1,0:T(8,128)(2,1)S(1)}, bf16[2,4,144,128]{3,2,1,0:T(8,128)(2,1)S(1)}, u32[]{:S(2)}, u32[]{:S(2)}) collective-permute-start(bf16[2,4,144,128]{3,2,1,0:T(8,128)(2,1)S(1)} %get-tuple-element.81), channel_id=1, source_target_pairs={{0,2},{1,3},{2,4},{3,5},{4,6},{5,7},{6,0},{7,1},{8,10},{9,11},{10,... | collective-permute-start | bytes 884744 | tf_op jit(solution)/shard_map/ppermute | solution.py:41
  179.1 8.1 %collective-permute-start.29 = (bf16[2,4,144,128]{3,2,1,0:T(8,128)(2,1)S(1)}, bf16[2,4,144,128]{3,2,1,0:T(8,128)(2,1)S(1)}, u32[]{:S(2)}, u32[]{:S(2)}) collective-permute-start(bf16[2,4,144,128]{3,2,1,0:T(8,128)(2,1)S(1)} %get-tuple-element.82), channel_id=1, source_target_pairs={{0,6},{1,7},{2,0},{3,1},{4,2},{5,3},{6,4},{7,5},{8,14},{9,15},{10,... | collective-permute-start | bytes 884744 | tf_op jit(solution)/shard_map/ppermute | solution.py:41
  181.5 10.8 %collective-permute-start.30 = (bf16[2,4,144,128]{3,2,1,0:T(8,128)(2,1)S(1)}, bf16[2,4,144,128]{3,2,1,0:T(8,128)(2,1)S(1)}, u32[]{:S(2)}, u32[]{:S(2)}) collective-permute-start(bf16[2,4,144,128]{3,2,1,0:T(8,128)(2,1)S(1)} %get-tuple-element.83), channel_id=1, source_target_pairs={{0,4},{1,5},{2,6},{3,7},{4,0},{5,1},{6,2},{7,3},{8,12},{9,13},{10,... | collective-permute-start | bytes 884744 | tf_op jit(solution)/shard_map/ppermute | solution.py:41
  192.3 4.6 %copy-start.4 = (bf16[2,6,128,128]{3,2,1,0:T(8,128)(2,1)}, bf16[2,6,128,128]{3,2,1,0:T(8,128)(2,1)S(1)}, u32[]{:S(2)}) copy-start(bf16[2,6,128,128]{3,2,1,0:T(8,128)(2,1)S(1)} %collective-permute-done.36.c_ref) | copy-start | bytes 1179652
  192.4 7.6 %collective-permute-start.37 = (bf16[2,6,128,128]{3,2,1,0:T(8,128)(2,1)S(1)}, bf16[2,6,128,128]{3,2,1,0:T(8,128)(2,1)S(1)}, u32[]{:S(2)}, u32[]{:S(2)}) collective-permute-start(bf16[2,6,128,128]{3,2,1,0:T(8,128)(2,1)S(1)} %pad_maximum_fusion.6), channel_id=1, source_target_pairs={{0,1},{1,0},{2,3},{3,2},{4,5},{5,4},{6,7},{7,6},{8,9},{9,8},{10,11... | collective-permute-start | bytes 1179656 | tf_op jit(solution)/shard_map/ppermute | solution.py:33
  200.0 0.8 copy-start.8

commit v2 on v1

--- a/solution.py
+++ b/solution.py
@@ -324,11 +324,16 @@
     def _():
         gacc[...] = mm(att_all[...], ub[...], ((0,), (0,)))
         for step, s in enumerate(ORDER):
-            places = {2: ((0, 0), (1, 16)), 1: ((2, 0), (0, 16)), 3: ((1, 0), (3, 0)), 0: ((4, 0), (4, 16))}[s]
-
             def put(index, value):
-                at, offset = places[index // 16]
-                terms[at][offset + index % 16] = value.astype(jnp.bfloat16)
+                if s == 2:
+                    at, place = (0, index) if index < 16 else (1, index - 4)
+                elif s == 1:
+                    at, place = (2, index) if index < 20 else (0, index - 4)
+                elif s == 3:
+                    at, place = (1, index) if index < 12 else (3, index - 12)
+                else:
+                    at, place = 4, index
+                terms[at][place] = value.astype(jnp.bfloat16)
 
             term = mm(nb_all[:, s * 512:(s + 1) * 512], dq_all[...], ((0,), (0,)))
             for k in range(4):
@@ -346,7 +351,7 @@
 
 
 def window_pass(scalars, xs, us, ws):
-    sizes = [32, 32, 16, 16, 32]
+    sizes = [28, 28, 20, 20, 32]
     dtypes = [jnp.bfloat16] * 5
     tile = pl.BlockSpec((4, 1, 2, WTOK, 128), lambda i, s: (0, i // 2, (i % 2) ^ s[0], 0, 0))
     part_specs = [
@@ -444,13 +449,15 @@
     low = [across(own[..., HALF:, :].astype(jnp.bfloat16), False), across(other[..., HALF:, :], True)]
 
     high, low = after((other[..., :HALF, :], plus(*low)), *low)
-    up, down = after((plus(up, lower[:16]), plus(down, upper[16:])), lower, upper, high, low)
+    up = jnp.concatenate([plus(up[:16], lower[:16]), up[16:]])
+    down = jnp.concatenate([down[:4], plus(down[4:], upper[12:])])
+    up, down = after((up, down), lower, upper, high, low)
     high = (own[..., :HALF, :] + swap_x(high).astype(jnp.float32)).astype(jnp.bfloat16)
     low = hop_z(low, 1)
     up, down = shift_y(up, -1), shift_y(down, 1)
 
     total = mine.astype(jnp.float32) + jnp.concatenate([up, lower[16:]]).astype(jnp.float32) + jnp.concatenate(
-        [upper[:16], down]).astype(jnp.float32)
+        [upper[:12], down]).astype(jnp.float32)
     full = jnp.concatenate([high, low], axis=3)
     (total,) = after((total,), full)
     back = [full[0]] + [shift_y(full[s], -s) for s in (1, 2, 3)]

time: 205 us -> 204 us (level)
    ppermute x5, waiting for transfers between devices: 5.92 us -> 13.5 us  [swap_x(): lax.ppermute(value, 'lon', [(lon_of(x, y, c), lon_of(1 - x, y, c)) for x,...]
    ppermute x14, waiting for transfers between devices: 51.9 us -> 45.4 us  [shift_y(): lax.ppermute(value, 'lon', [(lon_of(x, y, c), lon_of(x, (y + by) % NY, c)...]
    ppermute x3, waiting for transfers between devices: 2.88 us -> 0.56 us  [hop_z(): return lax.ppermute(value, ('lat', 'lon'), pairs)]
  transfers between devices with their start and end apart: 38 -> 38, of which waited for: 24 -> 23; matrix products, arithmetic and copies ran while one was open for 8% -> 8% of each run, Pallas kernels for 1% -> 1%
where the time goes in v2:
time: 204 us; the launch traced here: 203 us
  waiting for transfers between devices  77.7 us (38%)
  starting transfers between devices  69.5 us (34%)
  Pallas kernels  36.1 us (18%)
  local copies, waits for them, and re-layouts  10.3 us (5%)
  other arithmetic  8.29 us (4%)
    ppermute x14, waiting for transfers between devices, shift_y(): lax.ppermute(value, 'lon', [(lon_of(x, y, c), lon_of(x, (y + by) % NY, c)...  45.4 us
    ppermute x9, starting transfers between devices, swap_c(): lax.ppermute(value, 'lon', [(lon_of(x, y, c), lon_of(x, y, 1 - c)) for x,...  26.8 us
    pallas_call x1, Pallas kernels, window_pass(): pl.pallas_call(window_kernel, grid_spec=pltpu.PrefetchScalarGridSpec(num_...  26.8 us
    ppermute x14, starting transfers between devices, shift_y(): lax.ppermute(value, 'lon', [(lon_of(x, y, c), lon_of(x, (y + by) % NY, c)...  13.6 us
    ppermute x5, waiting for transfers between devices, swap_x(): lax.ppermute(value, 'lon', [(lon_of(x, y, c), lon_of(1 - x, y, c)) for x,...  13.5 us
    ppermute x3, starting transfers between devices, hop_z(): return lax.ppermute(value, ('lat', 'lon'), pairs)  12.2 us
    ppermute x6, waiting for transfers between devices, across(): return lax.ppermute(value, ('lat', 'lon'), pairs)  11 us
    ppermute x5, starting transfers between devices, swap_x(): lax.ppermute(value, 'lon', [(lon_of(x, y, c), lon_of(1 - x, y, c)) for x,...  9.04 us
  transfers between devices with their start and end apart: 38, of which 23 were waited for; matrix products, arithmetic and copies ran while one was open for 8% of the time, Pallas kernels for 1%

profile of v2, /device:TPU:1, one launch (start us, length us, event | category | flops | bytes accessed | tf_op | source)
XLA Modules:
  0.0 203.0 jit_solution(10204323731958484088)
XLA Ops:
  0.7 0.6 pad_add_fusion.s_ref
  1.3 3.1 %weight_split.1 = (bf16[4,6,128,128]{3,2,1,0:T(8,128)(2,1)}, bf16[8,128,128]{2,1,0:T(8,128)(2,1)}) custom-call(s32[4]{0:T(128)} %pad_add_fusion.s_ref, bf16[128,3072]{1,0:T(8,128)(2,1)} %q_ref.1, bf16[64,2048]{1,0:T(8,128)(2,1)} %o_ref.1), custom_call_target="tpu_custom_call" | custom-call | bytes 2000000 | tf_op jit(solution)/shard_map/weight_split/pallas_call | solution.py:93
  4.4 1.2 slice.144
  5.6 1.5 collective-permute-start.2
  7.1 1.2 slice.147
  8.4 5.7 %collective-permute-start.3 = (bf16[6,192,2,128]{3,2,1,0:T(2,128)(2,1)}, bf16[6,192,2,128]{3,2,1,0:T(2,128)(2,1)S(1)}, u32[]{:S(2)}, u32[]{:S(2)}) collective-permute-start(bf16[6,192,2,128]{3,2,1,0:T(2,128)(2,1)} %slice.147), channel_id=1, source_target_pairs={{0,96},{1,97},{2,98},{3,99},{4,100},{5,101},{6,102},{7,103},{8,104... | collective-permute-start | bytes 1769480 | tf_op jit(solution)/shard_map/ppermute | solution.py:49
  14.2 2.8 %collective-permute-start = (bf16[2,6,128,128]{3,2,1,0:T(8,128)(2,1)S(1)}, bf16[2,6,128,128]{3,2,1,0:T(8,128)(2,1)S(1)}, u32[]{:S(2)}, u32[]{:S(2)}) collective-permute-start(bf16[2,6,128,128]{3,2,1,0:T(8,128)(2,1)S(1)} %stack.39), channel_id=1, source_target_pairs={{0,8},{1,9},{2,10},{3,11},{4,12},{5,13},{6,14},{7,15},{8,0},{9,1},... | collective-permute-start | bytes 1179656 | tf_op jit(solution)/shard_map/ppermute | solution.py:37
  17.0 0.7 slice_bitcast_fusion.4
  17.7 1.5 pad_maximum_fusion.1
  19.2 1.0 copy.10
  20.2 2.5 %collective-permute-done = bf16[2,6,128,128]{3,2,1,0:T(8,128)(2,1)S(1)} collective-permute-done((bf16[2,6,128,128]{3,2,1,0:T(8,128)(2,1)S(1)}, bf16[2,6,128,128]{3,2,1,0:T(8,128)(2,1)S(1)}, u32[]{:S(2)}, u32[]{:S(2)}) %collective-permute-start) | collective-permute-done | bytes 393248 | tf_op jit(solution)/shard_map/ppermute | solution.py:37
  22.7 0.7 slice_bitcast_fusion.3
  23.4 0.8 pad_maximum_fusion.7
  24.2 6.0 %collective-permute-start.1 = (bf16[2,6,128,128]{3,2,1,0:T(8,128)(2,1)}, bf16[2,6,128,128]{3,2,1,0:T(8,128)(2,1)}, u32[]{:S(2)}, u32[]{:S(2)}) collective-permute-start(bf16[2,6,128,128]{3,2,1,0:T(8,128)(2,1)} %pad_maximum_fusion.7), channel_id=1, source_target_pairs={{0,1},{1,0},{2,3},{3,2},{4,5},{5,4},{6,7},{7,6},{8,9},{9,8},{10,11... | collective-permute-start | bytes 1179656 | tf_op jit(solution)/shard_map/ppermute | solution.py:33
  30.2 1.0 fusion.10
  31.9 0.9 token_split.1
  32.8 2.5 %collective-permute-start.6 = (bf16[2,2,4,6,6,2,128]{6,5,4,3,2,1,0:T(2,128)(2,1)S(1)}, bf16[2,2,4,6,6,2,128]{6,5,4,3,2,1,0:T(2,128)(2,1)S(1)}, u32[]{:S(2)}, u32[]{:S(2)}) collective-permute-start(bf16[2,2,4,6,6,2,128]{6,5,4,3,2,1,0:T(2,128)(2,1)S(1)} %get-tuple-element.51), channel_id=1, source_target_pairs={{0,4},{1,5},{2,6},{3,7},{4,0},{5,1},{6,2},{7,3},{8,12},{9,13},{10,... | collective-permute-start | bytes 884744 | tf_op jit(solution)/shard_map/ppermute | solution.py:41
  35.3 1.1 collective-permute-start.7
  36.4 2.0 collective-permute-start.4
  38.6 2.8 %collective-permute-start.8 = (bf16[2,72,2048]{2,1,0:T(8,128)(2,1)S(1)}, bf16[2,72,2048]{2,1,0:T(8,128)(2,1)S(1)}, u32[]{:S(2)}, u32[]{:S(2)}) collective-permute-start(bf16[2,72,2048]{2,1,0:T(8,128)(2,1)S(1)} %squeeze.26), channel_id=1, source_target_pairs={{0,8},{1,9},{2,10},{3,11},{4,12},{5,13},{6,14},{7,15},{8,0},{9,1},... | collective-permute-start | bytes 1769480 | tf_op jit(solution)/shard_map/ppermute | solution.py:37
  41.5 1.1 pad_maximum_fusion.2.refs_12_
  43.1 5.8 %collective-permute-done.6 = bf16[2,2,4,6,6,2,128]{6,5,4,3,2,1,0:T(2,128)(2,1)S(1)} collective-permute-done((bf16[2,2,4,6,6,2,128]{6,5,4,3,2,1,0:T(2,128)(2,1)S(1)}, bf16[2,2,4,6,6,2,128]{6,5,4,3,2,1,0:T(2,128)(2,1)S(1)}, u32[]{:S(2)}, u32[]{:S(2)}) %collective-permute-start.6) | collective-permute-done | bytes 294944 | tf_op jit(solution)/shard_map/ppermute | solution.py:41
  49.5 2.2 %pad_maximum_fusion.5 = (bf16[4,2,4,6,6,2,128]{6,5,4,3,2,1,0:T(2,128)(2,1)S(1)}, bf16[4,2,4,6,6,2,128]{6,5,4,3,2,1,0:T(2,128)(2,1)S(1)}) fusion(bf16[1,2,4,6,6,2,128]{6,5,4,3,2,1,0:T(2,128)(2,1)S(1)} %get-tuple-element.100, bf16[1,2,4,6,6,2,128]{6,5,4,3,2,1,0:T(2,128)(2,1)S(1)} %get-tuple-element.98, ...), kind=kLoop, calls=%fused_computation.26 | loop fusion | flops 1769472 | bytes 2359296 | tf_op jit(solution)/shard_map/stack | solution.py:416
  51.7 0.6 collective-permute-done.4
  52.3 1.0 collective-permute-done.8
  53.2 1.5 collective-permute-start.12
  54.8 3.0 %collective-permute-start.13 = (bf16[2,72,2048]{2,1,0:T(8,128)(2,1)S(1)}, bf16[2,72,2048]{2,1,0:T(8,128)(2,1)S(1)}, u32[]{:S(2)}, u32[]{:S(2)}) collective-permute-start(bf16[2,72,2048]{2,1,0:T(8,128)(2,1)S(1)} %collective-permute-done.4), channel_id=1, source_target_pairs={{0,24},{1,25},{2,26},{3,27},{4,28},{5,29},{6,30},{7,31},{8,16},{9,... | collective-permute-start | bytes 1769480 | tf_op jit(solution)/shard_map/ppermute | solution.py:58
  58.1 9.5 %collective-permute-done.14 = bf16[2,72,2048]{2,1,0:T(8,128)(2,1)S(1)} collective-permute-done((bf16[2,72,2048]{2,1,0:T(8,128)(2,1)S(1)}, bf16[2,72,2048]{2,1,0:T(8,128)(2,1)S(1)}, u32[]{:S(2)}, u32[]{:S(2)}) %collective-permute-start.14) | collective-permute-done | bytes 589856 | tf_op jit(solution)/shard_map/ppermute | solution.py:58
  67.7 5.6 %collective-permute-start.19 = (bf16[2,144,2048]{2,1,0:T(8,128)(2,1)S(1)}, bf16[2,144,2048]{2,1,0:T(8,128)(2,1)S(1)}, u32[]{:S(2)}, u32[]{:S(2)}) collective-permute-start(bf16[2,144,2048]{2,1,0:T(8,128)(2,1)S(1)} %constant_dynamic-update-slice_fusion.2.refs_8_), channel_id=1, source_target_pairs={{0,1},{1,0},{2,3},{3,2},{4,5},{5,4},{6,7},{7,6},{8,9},{9,8},{10,11... | collective-permute-start | bytes 3538952 | tf_op jit(solution)/shard_map/ppermute | solution.py:33
  73.3 2.2 %collective-permute-done.12.refs_15_ = bf16[32,128,128]{2,1,0:T(8,128)(2,1)S(1)} collective-permute-done((bf16[32,128,128]{2,1,0:T(8,128)(2,1)S(1)}, bf16[32,128,128]{2,1,0:T(8,128)(2,1)S(1)}, u32[]{:S(2)}, u32[]{:S(2)}) %collective-permute-start.12) | collective-permute-done | bytes 1048608 | tf_op jit(solution)/shard_map/ppermute | solution.py:41
  75.5 3.3 %collective-permute-start.9 = (bf16[4,2,4,72,128]{4,3,2,1,0:T(8,128)(2,1)S(1)}, bf16[4,2,4,72,128]{4,3,2,1,0:T(8,128)(2,1)S(1)}, u32[]{:S(2)}, u32[]{:S(2)}) collective-permute-start(bf16[4,2,4,72,128]{4,3,2,1,0:T(8,128)(2,1)S(1)} %bitcast.44), channel_id=1, source_target_pairs={{0,1},{1,0},{2,3},{3,2},{4,5},{5,4},{6,7},{7,6},{8,9},{9,8},{10,11... | collective-permute-start | bytes 1769480 | tf_op jit(solution)/shard_map/ppermute | solution.py:33
  78.9 2.4 %collective-permute-done.10.refs_2_ = bf16[4,2,4,72,128]{4,3,2,1,0:T(8,128)(2,1)S(1)} collective-permute-done((bf16[4,2,4,72,128]{4,3,2,1,0:T(8,128)(2,1)S(1)}, bf16[4,2,4,72,128]{4,3,2,1,0:T(8,128)(2,1)S(1)}, u32[]{:S(2)}, u32[]{:S(2)}) %collective-permute-start.10) | collective-permute-done | bytes 589856 | tf_op jit(solution)/shard_map/ppermute | solution.py:37
  81.3 1.4 collective-permute-start.16
  82.7 2.7 %collective-permute-start.18 = (bf16[16,128,128]{2,1,0:T(8,128)(2,1)S(1)}, bf16[16,128,128]{2,1,0:T(8,128)(2,1)S(1)}, u32[]{:S(2)}, u32[]{:S(2)}) collective-permute-start(bf16[16,128,128]{2,1,0:T(8,128)(2,1)S(1)} %slice.193), channel_id=1, source_target_pairs={{0,6},{1,7},{2,0},{3,1},{4,2},{5,3},{6,4},{7,5},{8,14},{9,15},{10,... | collective-permute-start | bytes 1572872 | tf_op jit(solution)/shard_map/ppermute | solution.py:41
  85.5 6.7 %collective-permute-done.17.refs_14_ = bf16[16,128,128]{2,1,0:T(8,128)(2,1)S(1)} collective-permute-done((bf16[16,128,128]{2,1,0:T(8,128)(2,1)S(1)}, bf16[16,128,128]{2,1,0:T(8,128)(2,1)S(1)}, u32[]{:S(2)}, u32[]{:S(2)}) %collective-permute-start.17) | collective-permute-done | bytes 524320 | tf_op jit(solution)/shard_map/ppermute | solution.py:41
  92.2 1.5 collective-permute-done.16.refs_6_
  93.8 7.1 %collective-permute-start.23 = (bf16[2,144,2048]{2,1,0:T(8,128)(2,1)S(1)}, bf16[2,144,2048]{2,1,0:T(8,128)(2,1)S(1)}, u32[]{:S(2)}, u32[]{:S(2)}) collective-permute-start(bf16[2,144,2048]{2,1,0:T(8,128)(2,1)S(1)} %constant_dynamic-update-slice_fusion.refs_10_), channel_id=1, source_target_pairs={{0,1},{1,0},{2,3},{3,2},{4,5},{5,4},{6,7},{7,6},{8,9},{9,8},{10,11... | collective-permute-start | bytes 3538952 | tf_op jit(solution)/shard_map/ppermute | solution.py:33
  101.5 2.7 %collective-permute-done.20.refs_3_ = bf16[4,2,4,72,128]{4,3,2,1,0:T(8,128)(2,1)S(1)} collective-permute-done((bf16[4,2,4,72,128]{4,3,2,1,0:T(8,128)(2,1)S(1)}, bf16[4,2,4,72,128]{4,3,2,1,0:T(8,128)(2,1)S(1)}, u32[]{:S(2)}, u32[]{:S(2)}) %collective-permute-start.20) | collective-permute-done | bytes 589856 | tf_op jit(solution)/shard_map/ppermute | solution.py:33
  104.2 0.8 collective-permute-done.21.refs_5_
  105.0 0.8 collective-permute-done.22.refs_7_
  105.9 26.8 %window_pass.1 = (bf16[2,4,2,4,144,128]{5,4,3,2,1,0:T(8,128)(2,1)S(1)}, bf16[4,2,4,144,128]{4,3,2,1,0:T(8,128)(2,1)S(1)}, bf16[4,2,4,144,128]{4,3,2,1,0:T(8,128)...) custom-call(s32[4]{0:T(128)S(1)} %copy-done.1, ...), custom_call_target="tpu_custom_call" | custom-call | flops 32000000000 | bytes 30000000 | tf_op jit(solution)/shard_map/window_pass/pallas_call | solution.py:363
  133.0 1.5 collective-permute-start.32
  134.5 2.8 %collective-permute-done.24 = bf16[2,4,2,4,144,128]{5,4,3,2,1,0:T(8,128)(2,1)S(1)} collective-permute-done((bf16[2,4,2,4,144,128]{5,4,3,2,1,0:T(8,128)(2,1)S(1)}, bf16[2,4,2,4,144,128]{5,4,3,2,1,0:T(8,128)(2,1)S(1)}, u32[]{:S(2)}, u32[]{:S(2)}) %collective-permute-start.24) | collective-permute-done | bytes 2359328 | tf_op jit(solution)/shard_map/ppermute | solution.py:33
  137.3 0.6 fusion
  137.9 1.8 collective-permute-start.25
  140.0 14.7 %collective-permute-done.32 = bf16[28,128,128]{2,1,0:T(8,128)(2,1)S(1)} collective-permute-done((bf16[28,128,128]{2,1,0:T(8,128)(2,1)S(1)}, bf16[28,128,128]{2,1,0:T(8,128)(2,1)S(1)}, u32[]{:S(2)}, u32[]{:S(2)}) %collective-permute-start.32) | collective-permute-done | bytes 917536 | tf_op jit(solution)/shard_map/ppermute | solution.py:41
  154.9 2.3 %collective-permute-done.33 = bf16[28,128,128]{2,1,0:T(8,128)(2,1)S(1)} collective-permute-done((bf16[28,128,128]{2,1,0:T(8,128)(2,1)S(1)}, bf16[28,128,128]{2,1,0:T(8,128)(2,1)S(1)}, u32[]{:S(2)}, u32[]{:S(2)}) %collective-permute-start.33) | collective-permute-done | bytes 917536 | tf_op jit(solution)/shard_map/ppermute | solution.py:41
  157.5 1.3 collective-permute-start.27
  158.9 0.6 collective-permute-start.34
  159.5 1.0 collective-permute-start.35
  160.4 4.4 %collective-permute-start.28 = (bf16[4,2,4,72,128]{4,3,2,1,0:T(8,128)(2,1)S(1)}, bf16[4,2,4,72,128]{4,3,2,1,0:T(8,128)(2,1)S(1)}, u32[]{:S(2)}, u32[]{:S(2)}) collective-permute-start(bf16[4,2,4,72,128]{4,3,2,1,0:T(8,128)(2,1)S(1)} %add_convert_fusion), channel_id=1, source_target_pairs={{0,32},{1,33},{2,34},{3,35},{4,36},{5,37},{6,38},{7,39},{8,40},{9,... | collective-permute-start | bytes 1769480 | tf_op jit(solution)/shard_map/ppermute | solution.py:49
  164.9 7.7 %collective-permute-done.27 = bf16[4,2,4,72,128]{4,3,2,1,0:T(8,128)(2,1)S(1)} collective-permute-done((bf16[4,2,4,72,128]{4,3,2,1,0:T(8,128)(2,1)S(1)}, bf16[4,2,4,72,128]{4,3,2,1,0:T(8,128)(2,1)S(1)}, u32[]{:S(2)}, u32[]{:S(2)}) %collective-permute-start.27) | collective-permute-done | bytes 589856 | tf_op jit(solution)/shard_map/ppermute | solution.py:37
  172.7 0.9 collective-permute-done.34
  173.6 1.7 collective-permute-done.35
  176.1 1.8 collective-permute-start.36
  178.1 2.7 %collective-permute-start.29 = (bf16[2,4,144,128]{3,2,1,0:T(8,128)(2,1)S(1)}, bf16[2,4,144,128]{3,2,1,0:T(8,128)(2,1)S(1)}, u32[]{:S(2)}, u32[]{:S(2)}) collective-permute-start(bf16[2,4,144,128]{3,2,1,0:T(8,128)(2,1)S(1)} %get-tuple-element.82), channel_id=1, source_target_pairs={{0,6},{1,7},{2,0},{3,1},{4,2},{5,3},{6,4},{7,5},{8,14},{9,15},{10,... | collective-permute-start | bytes 884744 | tf_op jit(solution)/shard_map/ppermute | solution.py:41
  180.8 4.6 %collective-permute-done.31 = bf16[2,4,144,128]{3,2,1,0:T(8,128)(2,1)S(1)} collective-permute-done((bf16[2,4,144,128]{3,2,1,0:T(8,128)(2,1)S(1)}, bf16[2,4,144,128]{3,2,1,0:T(8,128)(2,1)S(1)}, u32[]{:S(2)}, u32[]{:S(2)}) %collective-permute-start.31) | collective-permute-done | bytes 294944 | tf_op jit(solution)/shard_map/ppermute | solution.py:41
  185.4 1.2 collective-permute-done.29
  186.5 4.8 %collective-permute-done.30 = bf16[2,4,144,128]{3,2,1,0:T(8,128)(2,1)S(1)} collective-permute-done((bf16[2,4,144,128]{3,2,1,0:T(8,128)(2,1)S(1)}, bf16[2,4,144,128]{3,2,1,0:T(8,128)(2,1)S(1)}, u32[]{:S(2)}, u32[]{:S(2)}) %collective-permute-start.30) | collective-permute-done | bytes 294944 | tf_op jit(solution)/shard_map/ppermute | solution.py:41
  191.3 3.9 %collective-permute-start.37 = (bf16[2,6,128,128]{3,2,1,0:T(8,128)(2,1)S(1)}, bf16[2,6,128,128]{3,2,1,0:T(8,128)(2,1)S(1)}, u32[]{:S(2)}, u32[]{:S(2)}) collective-permute-start(bf16[2,6,128,128]{3,2,1,0:T(8,128)(2,1)S(1)} %pad_maximum_fusion.8), channel_id=1, source_target_pairs={{0,1},{1,0},{2,3},{3,2},{4,5},{5,4},{6,7},{7,6},{8,9},{9,8},{10,11... | collective-permute-start | bytes 1179656 | tf_op jit(solution)/shard_map/ppermute | solution.py:33
  195.7 1.2 broadcast_in_dim_reshape.3
  196.9 1.9 token_join.1
  198.8 0.7 copy-done.9
  199.5 3.5 %weight_join.1 = f32[128,3072]{1,0:T(8,128)} custom-call(s32[4]{0:T(128)} %pad_add_fusion.s_ref, f32[32,128,128]{2,1,0:T(8,128)} %copy-done.2, bf16[2,6,128,128]{3,2,1,0:T(8,128)(2,1)} %copy-done.9, bf16[2,6,128,128]{3,2,1,0:T(8,128)(2,1)} %copy-done.5), custom_call_target="tpu_custom_call" | custom-call | bytes 3000000 | tf_op jit(solution)/shard_map/weight_join/pallas_call | solution.py:126
  (90 shorter events, 6.0 us)
Async XLA Ops:
  0.6 6.5 %copy-start = (bf16[12,192,2,128]{3,2,1,0:T(2,128)(2,1)S(1)}, bf16[12,192,2,128]{3,2,1,0:T(2,128)(2,1)}, u32[]{:S(2)}) copy-start(bf16[12,192,2,128]{3,2,1,0:T(2,128)(2,1)} %high_ref.1) | copy-start | bytes 3538948
  4.4 9.7 %copy-start.6 = (bf16[4,6,128,128]{3,2,1,0:T(8,128)(2,1)S(1)}, bf16[4,6,128,128]{3,2,1,0:T(8,128)(2,1)}, u32[]{:S(2)}) copy-start(bf16[4,6,128,128]{3,2,1,0:T(8,128)(2,1)} %get-tuple-element.41) | copy-start | bytes 2359300
  5.6 12.0 %collective-permute-start.2 = (bf16[12,3,2,2048]{3,2,1,0:T(2,128)(2,1)S(1)}, bf16[12,3,2,2048]{3,2,1,0:T(2,128)(2,1)S(1)}, u32[]{:S(2)}, u32[]{:S(2)}) collective-permute-start(bf16[12,3,2,2048]{3,2,1,0:T(2,128)(2,1)S(1)} %slice.144), channel_id=1, source_target_pairs={{0,15},{1,0},{2,1},{3,2},{4,3},{5,4},{6,5},{7,6},{8,7},{9,8},{10,9... | collective-permute-start | bytes 884744 | tf_op jit(solution)/shard_map/ppermute | solution.py:62
  8.4 23.4 %collective-permute-start.3 = (bf16[6,192,2,128]{3,2,1,0:T(2,128)(2,1)}, bf16[6,192,2,128]{3,2,1,0:T(2,128)(2,1)S(1)}, u32[]{:S(2)}, u32[]{:S(2)}) collective-permute-start(bf16[6,192,2,128]{3,2,1,0:T(2,128)(2,1)} %slice.147), channel_id=1, source_target_pairs={{0,96},{1,97},{2,98},{3,99},{4,100},{5,101},{6,102},{7,103},{8,104... | collective-permute-start | bytes 1769480 | tf_op jit(solution)/shard_map/ppermute | solution.py:49
  14.1 3.5 %slice-start = ((bf16[12,12,2,2048]{3,2,1,0:T(2,128)(2,1)}), bf16[12,9,2,2048]{3,2,1,0:T(2,128)(2,1)S(1)}, s32[]{:S(2)}) async-start(bf16[12,12,2,2048]{3,2,1,0:T(2,128)(2,1)} %param.5), calls=%async_computation | async-start | bytes 1769472 | tf_op jit(solution)/shard_map/slice | solution.py:408
  14.2 8.6 %collective-permute-start = (bf16[2,6,128,128]{3,2,1,0:T(8,128)(2,1)S(1)}, bf16[2,6,128,128]{3,2,1,0:T(8,128)(2,1)S(1)}, u32[]{:S(2)}, u32[]{:S(2)}) collective-permute-start(bf16[2,6,128,128]{3,2,1,0:T(8,128)(2,1)S(1)} %stack.39), channel_id=1, source_target_pairs={{0,8},{1,9},{2,10},{3,11},{4,12},{5,13},{6,14},{7,15},{8,0},{9,1},... | collective-permute-start | bytes 1179656 | tf_op jit(solution)/shard_map/ppermute | solution.py:37
  24.2 14.4 %collective-permute-start.1 = (bf16[2,6,128,128]{3,2,1,0:T(8,128)(2,1)}, bf16[2,6,128,128]{3,2,1,0:T(8,128)(2,1)}, u32[]{:S(2)}, u32[]{:S(2)}) collective-permute-start(bf16[2,6,128,128]{3,2,1,0:T(8,128)(2,1)} %pad_maximum_fusion.7), channel_id=1, source_target_pairs={{0,1},{1,0},{2,3},{3,2},{4,5},{5,4},{6,7},{7,6},{8,9},{9,8},{10,11... | collective-permute-start | bytes 1179656 | tf_op jit(solution)/shard_map/ppermute | solution.py:33
  31.2 0.7 copy-start.1
  31.7 9.8 %copy-start.7 = (bf16[6,128,128]{2,1,0:T(8,128)(2,1)S(1)}, bf16[6,128,128]{2,1,0:T(8,128)(2,1)}, u32[]{:S(2)}) copy-start(bf16[6,128,128]{2,1,0:T(8,128)(2,1)} %get-tuple-element.89) | copy-start | bytes 589828
  31.7 9.7 %copy-start.8 = (bf16[6,128,128]{2,1,0:T(8,128)(2,1)S(1)}, bf16[6,128,128]{2,1,0:T(8,128)(2,1)}, u32[]{:S(2)}) copy-start(bf16[6,128,128]{2,1,0:T(8,128)(2,1)} %get-tuple-element.91) | copy-start | bytes 589828
  31.7 9.7 %copy-start.10 = (bf16[8,128,128]{2,1,0:T(8,128)(2,1)S(1)}, bf16[8,128,128]{2,1,0:T(8,128)(2,1)}, u32[]{:S(2)}) copy-start(bf16[8,128,128]{2,1,0:T(8,128)(2,1)} %get-tuple-element.42) | copy-start | bytes 786436
  32.8 10.1 %collective-permute-start.5 = (bf16[2,2,4,6,6,2,128]{6,5,4,3,2,1,0:T(2,128)(2,1)S(1)}, bf16[2,2,4,6,6,2,128]{6,5,4,3,2,1,0:T(2,128)(2,1)S(1)}, u32[]{:S(2)}, u32[]{:S(2)}) collective-permute-start(bf16[2,2,4,6,6,2,128]{6,5,4,3,2,1,0:T(2,128)(2,1)S(1)} %get-tuple-element.50), channel_id=1, source_target_pairs={{0,2},{1,3},{2,4},{3,5},{4,6},{5,7},{6,0},{7,1},{8,10},{9,11},{10,... | collective-permute-start | bytes 884744 | tf_op jit(solution)/shard_map/ppermute | solution.py:41
  32.8 16.0 %collective-permute-start.6 = (bf16[2,2,4,6,6,2,128]{6,5,4,3,2,1,0:T(2,128)(2,1)S(1)}, bf16[2,2,4,6,6,2,128]{6,5,4,3,2,1,0:T(2,128)(2,1)S(1)}, u32[]{:S(2)}, u32[]{:S(2)}) collective-permute-start(bf16[2,2,4,6,6,2,128]{6,5,4,3,2,1,0:T(2,128)(2,1)S(1)} %get-tuple-element.51), channel_id=1, source_target_pairs={{0,4},{1,5},{2,6},{3,7},{4,0},{5,1},{6,2},{7,3},{8,12},{9,13},{10,... | collective-permute-start | bytes 884744 | tf_op jit(solution)/shard_map/ppermute | solution.py:41
  35.3 14.0 %collective-permute-start.7 = (bf16[2,2,4,6,6,2,128]{6,5,4,3,2,1,0:T(2,128)(2,1)S(1)}, bf16[2,2,4,6,6,2,128]{6,5,4,3,2,1,0:T(2,128)(2,1)S(1)}, u32[]{:S(2)}, u32[]{:S(2)}) collective-permute-start(bf16[2,2,4,6,6,2,128]{6,5,4,3,2,1,0:T(2,128)(2,1)S(1)} %get-tuple-element.52), channel_id=1, source_target_pairs={{0,6},{1,7},{2,0},{3,1},{4,2},{5,3},{6,4},{7,5},{8,14},{9,15},{10,... | collective-permute-start | bytes 884744 | tf_op jit(solution)/shard_map/ppermute | solution.py:41
  36.4 15.9 %collective-permute-start.4 = (bf16[2,72,2048]{2,1,0:T(8,128)(2,1)S(1)}, bf16[2,72,2048]{2,1,0:T(8,128)(2,1)S(1)}, u32[]{:S(2)}, u32[]{:S(2)}) collective-permute-start(bf16[2,72,2048]{2,1,0:T(8,128)(2,1)S(1)} %squeeze.25), channel_id=1, source_target_pairs={{0,96},{1,97},{2,98},{3,99},{4,100},{5,101},{6,102},{7,103},{8,104... | collective-permute-start | bytes 1769480 | tf_op jit(solution)/shard_map/ppermute | solution.py:49
  38.6 14.6 %collective-permute-start.8 = (bf16[2,72,2048]{2,1,0:T(8,128)(2,1)S(1)}, bf16[2,72,2048]{2,1,0:T(8,128)(2,1)S(1)}, u32[]{:S(2)}, u32[]{:S(2)}) collective-permute-start(bf16[2,72,2048]{2,1,0:T(8,128)(2,1)S(1)} %squeeze.26), channel_id=1, source_target_pairs={{0,8},{1,9},{2,10},{3,11},{4,12},{5,13},{6,14},{7,15},{8,0},{9,1},... | collective-permute-start | bytes 1769480 | tf_op jit(solution)/shard_map/ppermute | solution.py:37
  53.2 22.3 %collective-permute-start.12 = (bf16[32,128,128]{2,1,0:T(8,128)(2,1)S(1)}, bf16[32,128,128]{2,1,0:T(8,128)(2,1)S(1)}, u32[]{:S(2)}, u32[]{:S(2)}) collective-permute-start(bf16[32,128,128]{2,1,0:T(8,128)(2,1)S(1)} %pad_maximum_fusion.2.refs_12_), channel_id=1, source_target_pairs={{0,6},{1,7},{2,0},{3,1},{4,2},{5,3},{6,4},{7,5},{8,14},{9,15},{10,... | collective-permute-start | bytes 3145736 | tf_op jit(solution)/shard_map/ppermute | solution.py:41
  54.8 12.9 %collective-permute-start.14 = (bf16[2,72,2048]{2,1,0:T(8,128)(2,1)S(1)}, bf16[2,72,2048]{2,1,0:T(8,128)(2,1)S(1)}, u32[]{:S(2)}, u32[]{:S(2)}) collective-permute-start(bf16[2,72,2048]{2,1,0:T(8,128)(2,1)S(1)} %collective-permute-done.4), channel_id=1, source_target_pairs={{0,16},{1,17},{2,18},{3,19},{4,20},{5,21},{6,22},{7,23},{8,24},{9,... | collective-permute-start | bytes 1769480 | tf_op jit(solution)/shard_map/ppermute | solution.py:58
  54.8 24.1 %collective-permute-start.11 = (bf16[32,128,128]{2,1,0:T(8,128)(2,1)S(1)}, bf16[32,128,128]{2,1,0:T(8,128)(2,1)S(1)}, u32[]{:S(2)}, u32[]{:S(2)}) collective-permute-start(bf16[32,128,128]{2,1,0:T(8,128)(2,1)S(1)} %pad_maximum_fusion.2.refs_12_), channel_id=1, source_target_pairs={{0,2},{1,3},{2,4},{3,5},{4,6},{5,7},{6,0},{7,1},{8,10},{9,11},{10,... | collective-permute-start | bytes 3145736 | tf_op jit(solution)/shard_map/ppermute | solution.py:41
  54.8 24.1 %collective-permute-start.13 = (bf16[2,72,2048]{2,1,0:T(8,128)(2,1)S(1)}, bf16[2,72,2048]{2,1,0:T(8,128)(2,1)S(1)}, u32[]{:S(2)}, u32[]{:S(2)}) collective-permute-start(bf16[2,72,2048]{2,1,0:T(8,128)(2,1)S(1)} %collective-permute-done.4), channel_id=1, source_target_pairs={{0,24},{1,25},{2,26},{3,27},{4,28},{5,29},{6,30},{7,31},{8,16},{9,... | collective-permute-start | bytes 1769480 | tf_op jit(solution)/shard_map/ppermute | solution.py:58
  57.8 23.4 %collective-permute-start.10 = (bf16[4,2,4,72,128]{4,3,2,1,0:T(8,128)(2,1)S(1)}, bf16[4,2,4,72,128]{4,3,2,1,0:T(8,128)(2,1)S(1)}, u32[]{:S(2)}, u32[]{:S(2)}) collective-permute-start(bf16[4,2,4,72,128]{4,3,2,1,0:T(8,128)(2,1)S(1)} %bitcast.43), channel_id=1, source_target_pairs={{0,8},{1,9},{2,10},{3,11},{4,12},{5,13},{6,14},{7,15},{8,0},{9,1},... | collective-permute-start | bytes 1769480 | tf_op jit(solution)/shard_map/ppermute | solution.py:37
  67.7 26.1 %collective-permute-start.19 = (bf16[2,144,2048]{2,1,0:T(8,128)(2,1)S(1)}, bf16[2,144,2048]{2,1,0:T(8,128)(2,1)S(1)}, u32[]{:S(2)}, u32[]{:S(2)}) collective-permute-start(bf16[2,144,2048]{2,1,0:T(8,128)(2,1)S(1)} %constant_dynamic-update-slice_fusion.2.refs_8_), channel_id=1, source_target_pairs={{0,1},{1,0},{2,3},{3,2},{4,5},{5,4},{6,7},{7,6},{8,9},{9,8},{10,11... | collective-permute-start | bytes 3538952 | tf_op jit(solution)/shard_map/ppermute | solution.py:33
  75.5 7.2 %collective-permute-start.9 = (bf16[4,2,4,72,128]{4,3,2,1,0:T(8,128)(2,1)S(1)}, bf16[4,2,4,72,128]{4,3,2,1,0:T(8,128)(2,1)S(1)}, u32[]{:S(2)}, u32[]{:S(2)}) collective-permute-start(bf16[4,2,4,72,128]{4,3,2,1,0:T(8,128)(2,1)S(1)} %bitcast.44), channel_id=1, source_target_pairs={{0,1},{1,0},{2,3},{3,2},{4,5},{5,4},{6,7},{7,6},{8,9},{9,8},{10,11... | collective-permute-start | bytes 1769480 | tf_op jit(solution)/shard_map/ppermute | solution.py:33
  81.3 12.5 %collective-permute-start.16 = (bf16[4,2,4,72,128]{4,3,2,1,0:T(8,128)(2,1)S(1)}, bf16[4,2,4,72,128]{4,3,2,1,0:T(8,128)(2,1)S(1)}, u32[]{:S(2)}, u32[]{:S(2)}) collective-permute-start(bf16[4,2,4,72,128]{4,3,2,1,0:T(8,128)(2,1)S(1)} %bitcast.53), channel_id=1, source_target_pairs={{0,24},{1,25},{2,26},{3,27},{4,28},{5,29},{6,30},{7,31},{8,16},{9,... | collective-permute-start | bytes 1769480 | tf_op jit(solution)/shard_map/ppermute | solution.py:58
  82.7 11.1 %collective-permute-start.15 = (bf16[4,2,4,72,128]{4,3,2,1,0:T(8,128)(2,1)S(1)}, bf16[4,2,4,72,128]{4,3,2,1,0:T(8,128)(2,1)S(1)}, u32[]{:S(2)}, u32[]{:S(2)}) collective-permute-start(bf16[4,2,4,72,128]{4,3,2,1,0:T(8,128)(2,1)S(1)} %bitcast.54), channel_id=1, source_target_pairs={{0,16},{1,17},{2,18},{3,19},{4,20},{5,21},{6,22},{7,23},{8,24},{9,... | collective-permute-start | bytes 1769480 | tf_op jit(solution)/shard_map/ppermute | solution.py:58
  82.7 9.5 %collective-permute-start.17 = (bf16[16,128,128]{2,1,0:T(8,128)(2,1)S(1)}, bf16[16,128,128]{2,1,0:T(8,128)(2,1)S(1)}, u32[]{:S(2)}, u32[]{:S(2)}) collective-permute-start(bf16[16,128,128]{2,1,0:T(8,128)(2,1)S(1)} %slice.192), channel_id=1, source_target_pairs={{0,2},{1,3},{2,4},{3,5},{4,6},{5,7},{6,0},{7,1},{8,10},{9,11},{10,... | collective-permute-start | bytes 1572872 | tf_op jit(solution)/shard_map/ppermute | solution.py:41
  82.7 9.5 %collective-permute-start.18 = (bf16[16,128,128]{2,1,0:T(8,128)(2,1)S(1)}, bf16[16,128,128]{2,1,0:T(8,128)(2,1)S(1)}, u32[]{:S(2)}, u32[]{:S(2)}) collective-permute-start(bf16[16,128,128]{2,1,0:T(8,128)(2,1)S(1)} %slice.193), channel_id=1, source_target_pairs={{0,6},{1,7},{2,0},{3,1},{4,2},{5,3},{6,4},{7,5},{8,14},{9,15},{10,... | collective-permute-start | bytes 1572872 | tf_op jit(solution)/shard_map/ppermute | solution.py:41
  93.8 12.1 %collective-permute-start.23 = (bf16[2,144,2048]{2,1,0:T(8,128)(2,1)S(1)}, bf16[2,144,2048]{2,1,0:T(8,128)(2,1)S(1)}, u32[]{:S(2)}, u32[]{:S(2)}) collective-permute-start(bf16[2,144,2048]{2,1,0:T(8,128)(2,1)S(1)} %constant_dynamic-update-slice_fusion.refs_10_), channel_id=1, source_target_pairs={{0,1},{1,0},{2,3},{3,2},{4,5},{5,4},{6,7},{7,6},{8,9},{9,8},{10,11... | collective-permute-start | bytes 3538952 | tf_op jit(solution)/shard_map/ppermute | solution.py:33
  100.9 3.3 %collective-permute-start.20 = (bf16[4,2,4,72,128]{4,3,2,1,0:T(8,128)(2,1)S(1)}, bf16[4,2,4,72,128]{4,3,2,1,0:T(8,128)(2,1)S(1)}, u32[]{:S(2)}, u32[]{:S(2)}) collective-permute-start(bf16[4,2,4,72,128]{4,3,2,1,0:T(8,128)(2,1)S(1)} %collective-permute-done.10.refs_2_), channel_id=1, source_target_pairs={{0,1},{1,0},{2,3},{3,2},{4,5},{5,4},{6,7},{7,6},{8,9},{9,8},{10,11... | collective-permute-start | bytes 1769480 | tf_op jit(solution)/shard_map/ppermute | solution.py:33
  101.0 4.1 %collective-permute-start.21 = (bf16[4,2,4,72,128]{4,3,2,1,0:T(8,128)(2,1)S(1)}, bf16[4,2,4,72,128]{4,3,2,1,0:T(8,128)(2,1)S(1)}, u32[]{:S(2)}, u32[]{:S(2)}) collective-permute-start(bf16[4,2,4,72,128]{4,3,2,1,0:T(8,128)(2,1)S(1)} %collective-permute-done.15.refs_4_), channel_id=1, source_target_pairs={{0,1},{1,0},{2,3},{3,2},{4,5},{5,4},{6,7},{7,6},{8,9},{9,8},{10,11... | collective-permute-start | bytes 1769480 | tf_op jit(solution)/shard_map/ppermute | solution.py:33
  101.4 4.5 %collective-permute-start.22 = (bf16[4,2,4,72,128]{4,3,2,1,0:T(8,128)(2,1)S(1)}, bf16[4,2,4,72,128]{4,3,2,1,0:T(8,128)(2,1)S(1)}, u32[]{:S(2)}, u32[]{:S(2)}) collective-permute-start(bf16[4,2,4,72,128]{4,3,2,1,0:T(8,128)(2,1)S(1)} %collective-permute-done.16.refs_6_), channel_id=1, source_target_pairs={{0,1},{1,0},{2,3},{3,2},{4,5},{5,4},{6,7},{7,6},{8,9},{9,8},{10,11... | collective-permute-start | bytes 1769480 | tf_op jit(solution)/shard_map/ppermute | solution.py:33
  132.7 4.6 %collective-permute-start.24 = (bf16[2,4,2,4,144,128]{5,4,3,2,1,0:T(8,128)(2,1)S(1)}, bf16[2,4,2,4,144,128]{5,4,3,2,1,0:T(8,128)(2,1)S(1)}, u32[]{:S(2)}, u32[]{:S(2)}) collective-permute-start(bf16[2,4,2,4,144,128]{5,4,3,2,1,0:T(8,128)(2,1)S(1)} %get-tuple-element.66), channel_id=1, source_target_pairs={{0,1},{1,0},{2,3},{3,2},{4,5},{5,4},{6,7},{7,6},{8,9},{9,8},{10,11... | collective-permute-start | bytes 7077896 | tf_op jit(solution)/shard_map/ppermute | solution.py:33
  133.0 21.7 %collective-permute-start.32 = (bf16[28,128,128]{2,1,0:T(8,128)(2,1)S(1)}, bf16[28,128,128]{2,1,0:T(8,128)(2,1)S(1)}, u32[]{:S(2)}, u32[]{:S(2)}) collective-permute-start(bf16[28,128,128]{2,1,0:T(8,128)(2,1)S(1)} %get-tuple-element.72), channel_id=1, source_target_pairs={{0,6},{1,7},{2,0},{3,1},{4,2},{5,3},{6,4},{7,5},{8,14},{9,15},{10,... | collective-permute-start | bytes 2752520 | tf_op jit(solution)/shard_map/ppermute | solution.py:41
  134.5 22.7 %collective-permute-start.33 = (bf16[28,128,128]{2,1,0:T(8,128)(2,1)S(1)}, bf16[28,128,128]{2,1,0:T(8,128)(2,1)S(1)}, u32[]{:S(2)}, u32[]{:S(2)}) collective-permute-start(bf16[28,128,128]{2,1,0:T(8,128)(2,1)S(1)} %get-tuple-element.74), channel_id=1, source_target_pairs={{0,2},{1,3},{2,4},{3,5},{4,6},{5,7},{6,0},{7,1},{8,10},{9,11},{10,... | collective-permute-start | bytes 2752520 | tf_op jit(solution)/shard_map/ppermute | solution.py:41
  137.9 19.4 %collective-permute-start.25 = (bf16[4,2,4,72,128]{4,3,2,1,0:T(8,128)(2,1)S(1)}, bf16[4,2,4,72,128]{4,3,2,1,0:T(8,128)(2,1)S(1)}, u32[]{:S(2)}, u32[]{:S(2)}) collective-permute-start(bf16[4,2,4,72,128]{4,3,2,1,0:T(8,128)(2,1)S(1)} %slice.261), channel_id=1, source_target_pairs={{0,16},{1,17},{2,18},{3,19},{4,20},{5,21},{6,22},{7,23},{8,24},{9,... | collective-permute-start | bytes 1769480 | tf_op jit(solution)/shard_map/ppermute | solution.py:58
  139.9 17.4 %collective-permute-start.26 = (bf16[4,2,4,72,128]{4,3,2,1,0:T(8,128)(2,1)S(1)}, bf16[4,2,4,72,128]{4,3,2,1,0:T(8,128)(2,1)S(1)}, u32[]{:S(2)}, u32[]{:S(2)}) collective-permute-start(bf16[4,2,4,72,128]{4,3,2,1,0:T(8,128)(2,1)S(1)} %get-tuple-element.85), channel_id=1, source_target_pairs={{0,24},{1,25},{2,26},{3,27},{4,28},{5,29},{6,30},{7,31},{8,16},{9,... | collective-permute-start | bytes 1769480 | tf_op jit(solution)/shard_map/ppermute | solution.py:58
  154.7 10.1 %copy-start.3 = (bf16[28,128,128]{2,1,0:T(8,128)(2,1)}, bf16[28,128,128]{2,1,0:T(8,128)(2,1)S(1)}, u32[]{:S(2)}) copy-start(bf16[28,128,128]{2,1,0:T(8,128)(2,1)S(1)} %collective-permute-done.32) | copy-start | bytes 2752516
  157.2 7.7 %copy-start.4 = (bf16[28,128,128]{2,1,0:T(8,128)(2,1)}, bf16[28,128,128]{2,1,0:T(8,128)(2,1)S(1)}, u32[]{:S(2)}) copy-start(bf16[28,128,128]{2,1,0:T(8,128)(2,1)S(1)} %collective-permute-done.33) | copy-start | bytes 2752516
  157.5 15.1 %collective-permute-start.27 = (bf16[4,2,4,72,128]{4,3,2,1,0:T(8,128)(2,1)S(1)}, bf16[4,2,4,72,128]{4,3,2,1,0:T(8,128)(2,1)S(1)}, u32[]{:S(2)}, u32[]{:S(2)}) collective-permute-start(bf16[4,2,4,72,128]{4,3,2,1,0:T(8,128)(2,1)S(1)} %get-tuple-element.68), channel_id=1, source_target_pairs={{0,8},{1,9},{2,10},{3,11},{4,12},{5,13},{6,14},{7,15},{8,0},{9,1},... | collective-permute-start | bytes 1769480 | tf_op jit(solution)/shard_map/ppermute | solution.py:37
  158.9 14.7 %collective-permute-start.34 = (bf16[20,128,128]{2,1,0:T(8,128)(2,1)S(1)}, bf16[20,128,128]{2,1,0:T(8,128)(2,1)S(1)}, u32[]{:S(2)}, u32[]{:S(2)}) collective-permute-start(bf16[20,128,128]{2,1,0:T(8,128)(2,1)S(1)} %pad_maximum_fusion.3), channel_id=1, source_target_pairs={{0,6},{1,7},{2,0},{3,1},{4,2},{5,3},{6,4},{7,5},{8,14},{9,15},{10,... | collective-permute-start | bytes 1966088 | tf_op jit(solution)/shard_map/ppermute | solution.py:41
  159.5 15.9 %collective-permute-start.35 = (bf16[20,128,128]{2,1,0:T(8,128)(2,1)S(1)}, bf16[20,128,128]{2,1,0:T(8,128)(2,1)S(1)}, u32[]{:S(2)}, u32[]{:S(2)}) collective-permute-start(bf16[20,128,128]{2,1,0:T(8,128)(2,1)S(1)} %pad_maximum_fusion.4), channel_id=1, source_target_pairs={{0,2},{1,3},{2,4},{3,5},{4,6},{5,7},{6,0},{7,1},{8,10},{9,11},{10,... | collective-permute-start | bytes 1966088 | tf_op jit(solution)/shard_map/ppermute | solution.py:41
  160.4 17.5 %collective-permute-start.28 = (bf16[4,2,4,72,128]{4,3,2,1,0:T(8,128)(2,1)S(1)}, bf16[4,2,4,72,128]{4,3,2,1,0:T(8,128)(2,1)S(1)}, u32[]{:S(2)}, u32[]{:S(2)}) collective-permute-start(bf16[4,2,4,72,128]{4,3,2,1,0:T(8,128)(2,1)S(1)} %add_convert_fusion), channel_id=1, source_target_pairs={{0,32},{1,33},{2,34},{3,35},{4,36},{5,37},{6,38},{7,39},{8,40},{9,... | collective-permute-start | bytes 1769480 | tf_op jit(solution)/shard_map/ppermute | solution.py:49
  164.9 10.5 %slice-start.1 = ((bf16[28,128,128]{2,1,0:T(8,128)(2,1)}), bf16[12,128,128]{2,1,0:T(8,128)(2,1)S(1)}, s32[]{:S(2)}) async-start(bf16[28,128,128]{2,1,0:T(8,128)(2,1)} %copy-done.3), calls=%async_computation.1 | async-start | bytes 786432 | tf_op jit(solution)/shard_map/slice | solution.py:459
  164.9 10.5 %slice-start.2 = ((bf16[28,128,128]{2,1,0:T(8,128)(2,1)}), bf16[12,128,128]{2,1,0:T(8,128)(2,1)S(1)}, s32[]{:S(2)}) async-start(bf16[28,128,128]{2,1,0:T(8,128)(2,1)} %copy-done.4), calls=%async_computation.2 | async-start | bytes 786432 | tf_op jit(solution)/shard_map/slice | solution.py:460
  175.9 19.3 %copy-start.2 = (f32[32,128,128]{2,1,0:T(8,128)}, f32[32,128,128]{2,1,0:T(8,128)S(1)}, u32[]{:S(2)}) copy-start(f32[32,128,128]{2,1,0:T(8,128)S(1)} %convert_add_fusion.2.a_ref) | copy-start | bytes 6291460
  176.1 15.2 %collective-permute-start.36 = (bf16[2,6,128,128]{3,2,1,0:T(8,128)(2,1)S(1)}, bf16[2,6,128,128]{3,2,1,0:T(8,128)(2,1)S(1)}, u32[]{:S(2)}, u32[]{:S(2)}) collective-permute-start(bf16[2,6,128,128]{3,2,1,0:T(8,128)(2,1)S(1)} %bitcast.55), channel_id=1, source_target_pairs={{0,8},{1,9},{2,10},{3,11},{4,12},{5,13},{6,14},{7,15},{8,0},{9,1},... | collective-permute-start | bytes 1179656 | tf_op jit(solution)/shard_map/ppermute | solution.py:37
  178.0 7.4 %collective-permute-start.31 = (bf16[2,4,144,128]{3,2,1,0:T(8,128)(2,1)S(1)}, bf16[2,4,144,128]{3,2,1,0:T(8,128)(2,1)S(1)}, u32[]{:S(2)}, u32[]{:S(2)}) collective-permute-start(bf16[2,4,144,128]{3,2,1,0:T(8,128)(2,1)S(1)} %get-tuple-element.81), channel_id=1, source_target_pairs={{0,2},{1,3},{2,4},{3,5},{4,6},{5,7},{6,0},{7,1},{8,10},{9,11},{10,... | collective-permute-start | bytes 884744 | tf_op jit(solution)/shard_map/ppermute | solution.py:41
  178.1 8.4 %collective-permute-start.29 = (bf16[2,4,144,128]{3,2,1,0:T(8,128)(2,1)S(1)}, bf16[2,4,144,128]{3,2,1,0:T(8,128)(2,1)S(1)}, u32[]{:S(2)}, u32[]{:S(2)}) collective-permute-start(bf16[2,4,144,128]{3,2,1,0:T(8,128)(2,1)S(1)} %get-tuple-element.82), channel_id=1, source_target_pairs={{0,6},{1,7},{2,0},{3,1},{4,2},{5,3},{6,4},{7,5},{8,14},{9,15},{10,... | collective-permute-start | bytes 884744 | tf_op jit(solution)/shard_map/ppermute | solution.py:41
  180.7 10.5 %collective-permute-start.30 = (bf16[2,4,144,128]{3,2,1,0:T(8,128)(2,1)S(1)}, bf16[2,4,144,128]{3,2,1,0:T(8,128)(2,1)S(1)}, u32[]{:S(2)}, u32[]{:S(2)}) collective-permute-start(bf16[2,4,144,128]{3,2,1,0:T(8,128)(2,1)S(1)} %get-tuple-element.83), channel_id=1, source_target_pairs={{0,4},{1,5},{2,6},{3,7},{4,0},{5,1},{6,2},{7,3},{8,12},{9,13},{10,... | collective-permute-start | bytes 884744 | tf_op jit(solution)/shard_map/ppermute | solution.py:41
  191.3 4.4 %copy-start.5 = (bf16[2,6,128,128]{3,2,1,0:T(8,128)(2,1)}, bf16[2,6,128,128]{3,2,1,0:T(8,128)(2,1)S(1)}, u32[]{:S(2)}) copy-start(bf16[2,6,128,128]{3,2,1,0:T(8,128)(2,1)S(1)} %collective-permute-done.36.c_ref) | copy-start | bytes 1179652
  191.3 7.4 %collective-permute-start.37 = (bf16[2,6,128,128]{3,2,1,0:T(8,128)(2,1)S(1)}, bf16[2,6,128,128]{3,2,1,0:T(8,128)(2,1)S(1)}, u32[]{:S(2)}, u32[]{:S(2)}) collective-permute-start(bf16[2,6,128,128]{3,2,1,0:T(8,128)(2,1)S(1)} %pad_maximum_fusion.8), channel_id=1, source_target_pairs={{0,1},{1,0},{2,3},{3,2},{4,5},{5,4},{6,7},{7,6},{8,9},{9,8},{10,11... | collective-permute-start | bytes 1179656 | tf_op jit(solution)/shard_map/ppermute | solution.py:33
  198.8 0.7 copy-start.9
